TPU v7x, 128 devices: a whole 4x4x4 slice. The times are simulated.
128 devices in a mesh: fsdp: 128 (over z, x, y, core).
Axes of the slice: x: 4, y: 4, z: 4, core: 2. Of those that a mesh axis runs over, the one named last changes fastest.
Arguments:
- inputs: bfloat16 [30720, 960], P('fsdp'), may hold values from -6 to 6
- cotangent: bfloat16 [30720, 960], P('fsdp'), may hold values from -16 to 16
- flat_weights: bfloat16 [9832320], P('fsdp')
- counts: int32 [384], P('fsdp'), may hold values from 40 to 80, as said below
- segments: int32 [30720], P('fsdp'), may hold values from -1 to 2, as said below
Outputs:
- block_out: bfloat16 [30720, 960], P('fsdp')
- input_grad: bfloat16 [30720, 960], P('fsdp')
- flat_grads: float32 [9832320], P('fsdp')
Inputs may be any that keep to these rules, and one draw needn't show every extreme that they name: `counts`: one micro-batch in every draw has all 80 rows live and another has exactly 40. `segments`: within a micro-batch the ids never fall over its live rows, which are its first counts rows; ids 0, 1 and 2 each mark one sequence; rows after the live ones hold -1.
All inputs are finite; a program needn't handle non-finite values.
Results may differ from a plain program's by a relative error of at most 0.011.
Values may be sent and summed in bfloat16 or wider, within the bound.
A program may use at most 256 MiB of HBM per device.

v0:
```python
import functools
import math

import jax
import jax.numpy as jnp
from jax import lax
from jax.experimental import pallas as pl
from jax.experimental.pallas import tpu as pltpu
from jax.sharding import PartitionSpec as P

D = 960
H = 15
KV = 5
HD = 64
FF = 2560
MB = 3
EPSILON = 1e-05
GAINS = 2 * D
BLOCK = 76800
N = 128
BF = jnp.bfloat16
F32 = jnp.float32

MESH = pl.DeviceIdType.MESH
TILES = 40
PARTS = ((0, 7, 14), (14, 20, 27), (27, 33, 40))


def place():
    me = lax.axis_index("fsdp")
    return [me // 32, (me // 8) % 4, (me // 2) % 4], me % 2


def device_at(coords, core):
    return (coords[0] * 32 + coords[1] * 8 + coords[2] * 2 + core,)


def moved(coords, dim, by):
    out = list(coords)
    out[dim] = (out[dim] + by + 4) % 4
    return out


def greet(coords, core):
    barrier = pltpu.get_barrier_semaphore()
    for dim in range(3):
        for by in (1, -1):
            pl.semaphore_signal(barrier, inc=1, device_id=device_at(moved(coords, dim, by), core), device_id_type=MESH)
    pl.semaphore_signal(barrier, inc=1, device_id=device_at(coords, 1 - core), device_id_type=MESH)
    pl.semaphore_wait(barrier, 7)


def gather_kernel(blk, out, send, recv, pair_send, pair_recv, own_sem):
    coords, core = place()
    greet(coords, core)
    sent = []

    def at(whole, fixed, tiles):
        index = [slice(None)] * 3
        for dim, value in fixed.items():
            index[dim] = value
        return whole.at[(*index, core, pl.ds(tiles[0], tiles[1] - tiles[0]))]

    def push(src, dst, device, ssem, rsem):
        copy = pltpu.make_async_remote_copy(src_ref=src, dst_ref=dst, send_sem=ssem, recv_sem=rsem, device_id=device, device_id_type=MESH)
        copy.start()
        sent.append(copy)

    def landed(dst, rsem):
        pltpu.make_async_copy(dst, dst, rsem).wait()

    own = {0: coords[0], 1: coords[1], 2: coords[2]}
    here = out.at[(*coords, core)]
    local = pltpu.make_async_copy(blk, here, own_sem)
    local.start()
    sibling = device_at(coords, 1 - core)
    push(blk, here, sibling, pair_send.at[36], pair_recv.at[36])

    def orders(p):
        return [(p + k) % 3 for k in range(3)]

    def halves(p, sign):
        lo, mid, hi = PARTS[p]
        first, second = (lo, mid), (mid, hi)
        return (first, second) if sign > 0 else (second, first)

    def fixed_at(p, phase, coord):
        fixed = {orders(p)[phase]: coord}
        for later in range(phase + 1, 3):
            fixed[orders(p)[later]] = coords[orders(p)[later]]
        return fixed

    def base(p, phase, sign):
        return ((p * 3 + phase) * 2 + (0 if sign > 0 else 1)) * 3

    def pair_base(p, phase):
        return (p * 3 + phase) * 4

    for phase in range(3):
        for half in range(2):
            for p in range(3):
                dim = orders(p)[phase]
                for sign in (1, -1):
                    tiles = halves(p, sign)[half]
                    ref = at(out, fixed_at(p, phase, coords[dim]), tiles)
                    src = blk.at[pl.ds(tiles[0], tiles[1] - tiles[0])] if phase == 0 else ref
                    k = base(p, phase, sign) + half
                    push(src, ref, device_at(moved(coords, dim, sign), core), send.at[k], recv.at[k])
        for p in range(3):
            dim = orders(p)[phase]
            for sign in (1, -1):
                tiles = halves(p, sign)[0]
                coord = moved(coords, dim, -sign)[dim]
                ref = at(out, fixed_at(p, phase, coord), tiles)
                k = base(p, phase, sign)
                landed(ref, recv.at[k])
                push(ref, ref, device_at(moved(coords, dim, sign), core), send.at[k + 2], recv.at[k + 2])
        for p in range(3):
            dim = orders(p)[phase]
            for n, sign in enumerate((1, -1)):
                tiles = halves(p, sign)[1]
                coord = moved(coords, dim, -sign)[dim]
                landed(at(out, fixed_at(p, phase, coord), tiles), recv.at[base(p, phase, sign) + 1])
                lo, mid, hi = PARTS[p]
                ref = at(out, fixed_at(p, phase, coord), (lo, hi))
                m = pair_base(p, phase) + n
                push(ref, ref, sibling, pair_send.at[m], pair_recv.at[m])
        for p in range(3):
            dim = orders(p)[phase]
            coord = moved(coords, dim, 2)[dim]
            for n, sign in enumerate((1, -1)):
                tiles = halves(p, sign)[0]
                ref = at(out, fixed_at(p, phase, coord), tiles)
                landed(ref, recv.at[base(p, phase, sign) + 2])
                m = pair_base(p, phase) + 2 + n
                push(ref, ref, sibling, pair_send.at[m], pair_recv.at[m])
        if phase == 0:
            local.wait()

    other = 1 - core

    def theirs(whole, fixed, tiles):
        index = [slice(None)] * 3
        for dim, value in fixed.items():
            index[dim] = value
        return whole.at[(*index, other, pl.ds(tiles[0], tiles[1] - tiles[0]))]

    landed(out.at[(*coords, other)], pair_recv.at[36])
    for phase in range(3):
        for p in range(3):
            dim = orders(p)[phase]
            lo, mid, hi = PARTS[p]
            for n, sign in enumerate((1, -1)):
                coord = moved(coords, dim, -sign)[dim]
                landed(theirs(out, fixed_at(p, phase, coord), (lo, hi)), pair_recv.at[pair_base(p, phase) + n])
            coord = moved(coords, dim, 2)[dim]
            for n, sign in enumerate((1, -1)):
                landed(theirs(out, fixed_at(p, phase, coord), halves(p, sign)[0]), pair_recv.at[pair_base(p, phase) + 2 + n])
    for copy in sent:
        copy.wait_send()


def gather(block):
    return pl.pallas_call(
        gather_kernel,
        out_shape=jax.ShapeDtypeStruct((4, 4, 4, 2, TILES, 16, 128), jnp.bfloat16),
        in_specs=[pl.BlockSpec(memory_space=pl.ANY)],
        out_specs=pl.BlockSpec(memory_space=pl.ANY),
        scratch_shapes=[
            pltpu.SemaphoreType.DMA((54,)),
            pltpu.SemaphoreType.DMA((54,)),
            pltpu.SemaphoreType.DMA((37,)),
            pltpu.SemaphoreType.DMA((37,)),
            pltpu.SemaphoreType.DMA,
        ],
        compiler_params=pltpu.CompilerParams(collective_id=0, has_side_effects=True),
    )(block)


def scatter_kernel(grads, out, mine, pair_buf, b1, b2, b3, send, recv, pair_send, pair_recv, own_sem):
    coords, core = place()
    greet(coords, core)
    other = 1 - core
    sibling = device_at(coords, other)
    bufs = (b1, b2, b3)
    sent = []

    def orders(p):
        return [(p + k) % 3 for k in range(3)]

    def index_of(fixed):
        index = [slice(None)] * 3
        for dim, value in fixed.items():
            index[dim] = value
        return tuple(index)

    def rng(tiles):
        return pl.ds(tiles[0], tiles[1] - tiles[0])

    def halves(p, sign):
        lo, mid, hi = PARTS[p]
        first, second = (lo, mid), (mid, hi)
        return (first, second) if sign > 0 else (second, first)

    def push(src, dst, device, ssem, rsem):
        copy = pltpu.make_async_remote_copy(src_ref=src, dst_ref=dst, send_sem=ssem, recv_sem=rsem, device_id=device, device_id_type=MESH)
        copy.start()
        sent.append(copy)

    def landed(dst, rsem):
        pltpu.make_async_copy(dst, dst, rsem).wait()

    order = (2, 1, -1, 0)
    local = {}
    for step in order:
        for p in range(3):
            dim = orders(p)[0]
            lo, mid, hi = PARTS[p]
            fixed = index_of({dim: moved(coords, dim, step)[dim]})
            k = p * 4 + step % 4
            push(grads.at[(*fixed, other, rng((lo, hi)))], pair_buf.at[(*fixed, rng((lo, hi)))], sibling, pair_send.at[k], pair_recv.at[k])
            copy = pltpu.make_async_copy(grads.at[(*fixed, core, rng((lo, hi)))], mine.at[(*fixed, rng((lo, hi)))], own_sem.at[k])
            copy.start()
            local[k] = copy

    def ready(p, step):
        dim = orders(p)[0]
        lo, mid, hi = PARTS[p]
        n = hi - lo
        coord = moved(coords, dim, step)[dim]
        fixed = index_of({dim: coord})
        k = p * 4 + step % 4
        local[k].wait()
        landed(pair_buf.at[(*fixed, rng((lo, hi)))], pair_recv.at[k])

        def body(t, _):
            index = [t // 4, t % 4]
            index.insert(dim, coord)
            where = (*index, rng((lo, hi)))
            mine[where] = mine[where] + pair_buf[where]
            return 0

        lax.fori_loop(0, 16, body, 0)

    def fixed_at(p, phase, coord):
        fixed = {}
        for earlier in range(phase):
            fixed[orders(p)[earlier]] = coords[orders(p)[earlier]]
        fixed[orders(p)[phase]] = coord
        return fixed

    def base(p, phase, sign):
        return ((p * 3 + phase) * 2 + (0 if sign > 0 else 1)) * 3

    def slot(phase, which, tiles):
        return bufs[phase].at[(which, *([slice(None)] * (2 - phase)), rng(tiles))]

    def ship(p, phase, sign, step, half, number):
        dim = orders(p)[phase]
        tiles = halves(p, sign)[half]
        fixed = index_of(fixed_at(p, phase, moved(coords, dim, step)[dim]))
        k = base(p, phase, sign) + number
        side = 0 if sign > 0 else 1
        which = 2 + side if number == 0 else side
        push(mine.at[(*fixed, rng(tiles))], slot(phase, which, tiles), device_at(moved(coords, dim, sign), core), send.at[k], recv.at[k])

    def loop(phase, p, coord, fn):
        dims = orders(p)
        if phase == 2:
            fn((*[coord if d == dims[2] else coords[d] for d in range(3)],), ())
            return
        free = [d for d in range(3) if d in dims[phase + 1:]]

        def body(t, _):
            inner = [t // 4, t % 4] if phase == 0 else [t]
            index = []
            for d in range(3):
                if d in free:
                    index.append(inner[free.index(d)])
                elif d == dims[phase]:
                    index.append(coord)
                else:
                    index.append(coords[d])
            fn(tuple(index), tuple(inner))
            return 0

        lax.fori_loop(0, 16 if phase == 0 else 4, body, 0)

    for phase in range(3):
        for p in range(3):
            if phase == 0:
                ready(p, 2)
            for sign in (1, -1):
                ship(p, phase, sign, 2, 0, 0)
        for p in range(3):
            for sign in (1, -1):
                if phase == 0:
                    ready(p, sign)
                ship(p, phase, sign, sign, 1, 1)
        for p in range(3):
            dim = orders(p)[phase]
            for side, sign in enumerate((1, -1)):
                tiles = halves(p, sign)[0]
                landed(slot(phase, 2 + side, tiles), recv.at[base(p, phase, sign)])
                coord = moved(coords, dim, sign)[dim]

                def fold(where, inner):
                    m = (*where, rng(tiles))
                    mine[m] = mine[m] + bufs[phase][(2 + side, *inner, rng(tiles))]

                loop(phase, p, coord, fold)
                ship(p, phase, sign, sign, 0, 2)
        for p in range(3):
            dim = orders(p)[phase]
            if phase == 0:
                ready(p, 0)
            for side, sign in enumerate((1, -1)):
                landed(slot(phase, side, halves(p, sign)[1]), recv.at[base(p, phase, sign) + 1])
                landed(slot(phase, side, halves(p, sign)[0]), recv.at[base(p, phase, sign) + 2])
            lo, mid, hi = PARTS[p]

            def total(where, inner):
                m = (*where, rng((lo, hi)))
                f = jnp.float32
                value = mine[m].astype(f) + bufs[phase][(0, *inner, rng((lo, hi)))].astype(f) + bufs[phase][(1, *inner, rng((lo, hi)))].astype(f)
                if phase == 2:
                    out[rng((lo, hi))] = value
                else:
                    mine[m] = value.astype(jnp.bfloat16)

            loop(phase, p, coords[dim], total)
    for copy in sent:
        copy.wait_send()


def scatter(grads):
    bf = jnp.bfloat16
    return pl.pallas_call(
        scatter_kernel,
        out_shape=jax.ShapeDtypeStruct((TILES, 16, 128), jnp.float32),
        in_specs=[pl.BlockSpec(memory_space=pl.ANY)],
        out_specs=pl.BlockSpec(memory_space=pltpu.VMEM),
        scratch_shapes=[
            pltpu.VMEM((4, 4, 4, TILES, 16, 128), bf),
            pltpu.VMEM((4, 4, 4, TILES, 16, 128), bf),
            pltpu.VMEM((4, 4, 4, TILES, 16, 128), bf),
            pltpu.VMEM((4, 4, TILES, 16, 128), bf),
            pltpu.VMEM((4, TILES, 16, 128), bf),
            pltpu.SemaphoreType.DMA((54,)),
            pltpu.SemaphoreType.DMA((54,)),
            pltpu.SemaphoreType.DMA((12,)),
            pltpu.SemaphoreType.DMA((12,)),
            pltpu.SemaphoreType.DMA((12,)),
        ],
        compiler_params=pltpu.CompilerParams(collective_id=1, has_side_effects=True, vmem_limit_bytes=60 * 1024 * 1024),
    )(grads)


def pack(rows_48, rows_80, rows_15, gains, d):
    qkv = jnp.pad(rows_48, ((0, 0), (0, 64))).reshape(3, 16, 13, 128).transpose(2, 0, 1, 3).reshape(39, 16, 128)
    qkv = jnp.concatenate([qkv, jnp.where(d == 0, gains, jnp.zeros_like(gains))[None]], axis=0)
    square = jnp.pad(rows_80, ((0, 0), (0, 64))).reshape(5, 16, 8, 128).transpose(2, 0, 1, 3).reshape(40, 16, 128)
    wide = jnp.pad(rows_15, ((0, 1), (0, 0))).reshape(16, 40, 128).transpose(1, 0, 2)
    return jnp.where(d < 20, qkv, jnp.where((d >= 32) & (d < 96), wide, square))


def to_block(shard, d):
    following = lax.ppermute(shard[:GAINS], "fsdp", [(i, (i + N - 1) % N) for i in range(N)])
    flat = lax.dynamic_slice(jnp.concatenate([shard, following]), (GAINS - 15 * d,), (BLOCK,))
    gains = jnp.pad(shard[:GAINS].reshape(2, D), ((0, 0), (0, 64))).reshape(16, 128)
    return pack(flat.reshape(48, 1600), flat.reshape(80, D), flat.reshape(15, 2 * FF), gains, d)


def from_block(tiles, d):
    qkv = tiles[:39].reshape(13, 3, 16, 128).transpose(1, 2, 0, 3).reshape(48, 1664)[:, :1600].reshape(-1)
    square = tiles.reshape(8, 5, 16, 128).transpose(1, 2, 0, 3).reshape(80, 1024)[:, :D].reshape(-1)
    wide = tiles.transpose(1, 0, 2)[:15].reshape(-1)
    flat = jnp.where(d < 20, qkv, jnp.where((d >= 32) & (d < 96), wide, square))
    before = lax.ppermute(flat[BLOCK - GAINS :], "fsdp", [(i, (i + 1) % N) for i in range(N)])
    before = jnp.where(d == 0, tiles[39].reshape(2, 1024)[:, :D].reshape(-1), before)
    return lax.dynamic_slice(jnp.concatenate([before, flat]), (15 * d,), (BLOCK + 15,))


ROWS = 240
MROWS = 80


def tables(segment_ids, counts):
    seg = segment_ids.reshape(MB, MROWS)
    places = jnp.arange(MROWS, dtype=jnp.int32)
    same = seg[:, :, None] == seg[:, None, :]
    first_row = jnp.min(jnp.where(same, places[None, None, :], MROWS), axis=2)
    position = (places[None, :] - first_row).astype(F32).reshape(ROWS)
    freq = jnp.exp(jnp.arange(HD // 2, dtype=F32) * (-2.0 * math.log(10000.0) / HD))
    angle = position[:, None] * freq[None, :]
    cos, sin = jnp.cos(angle), jnp.sin(angle)
    cos_t = jnp.concatenate([cos, cos, cos, cos], axis=1)
    sin_t = jnp.concatenate([-sin, sin, -sin, sin], axis=1)
    allowed = same & (places[None, None, :] <= places[None, :, None])
    bias = jnp.where(allowed, 0.0, -1e30).astype(F32).reshape(ROWS, MROWS)
    live = (places[None, :] < counts[:, None]).astype(F32).reshape(ROWS, 1)
    return cos_t, sin_t, bias, jnp.broadcast_to(live, (ROWS, 128))


def dot(a, b, ca=1, cb=0):
    return lax.dot_general(a, b, (((ca,), (cb,)), ((), ())), preferred_element_type=F32)


def mean_of(value):
    return jnp.sum(value, axis=-1, keepdims=True) * (1.0 / D)


def compute_kernel(
    blocks, x_ref, c_ref, cos_ref, sin_ref, bias_ref, live_ref,
    out_ref, gin_ref, terms,
    w, xs, go, nrm, qs, kk, vv, prob, mixed, mid, n2p, gate, up, hid, ggu, gq, gqb, spread, acc, in_sem, out_sem,
):
    spans = ((0, 20), (20, 32), (32, 96), (96, 128))

    def span(ref, i):
        return ref.at[pl.ds(spans[i][0], spans[i][1] - spans[i][0])]

    loads = [pltpu.make_async_copy(span(blocks, i), span(w, i), in_sem.at[i]) for i in range(4)]
    stores = [pltpu.make_async_copy(span(w, i), span(terms, i), out_sem.at[i]) for i in range(4)]
    for load in loads:
        load.start()

    def qkv_tiles(c):
        return w[0:20, 3 * c : 3 * c + 3].reshape(D, 128)

    def out_tiles(c):
        return w[20:32, 5 * c : 5 * c + 5].reshape(D, 128)

    def side(parts):
        return jnp.concatenate(parts, axis=1)

    def in_tiles(c):
        return side([w[32:96, 5 * c + i].reshape(1024, 128) for i in range(5)])

    def down_tiles(c):
        return side([w[pl.ds(96 + 8 * c, 8), 5 * i : 5 * i + 5].reshape(640, 128) for i in range(8)])

    lane = lax.broadcasted_iota(jnp.int32, (MROWS, 128), 1)
    half = (lane < 64, lane >= 64)
    lane_all = lax.broadcasted_iota(jnp.int32, (ROWS, 128), 1)
    low_all = lane_all < 64
    first_all = lane_all % 64 < 32

    def swap(v):
        return jnp.where(first_all, pltpu.roll(v, 96, 1), pltpu.roll(v, 32, 1))

    def both(v, h):
        other = pltpu.roll(v, 64, 1)
        return jnp.where(low_all, v, other) if h == 0 else jnp.where(low_all, other, v)

    r = lax.broadcasted_iota(jnp.int32, (1024, 1024), 0)
    c = lax.broadcasted_iota(jnp.int32, (1024, 1024), 1)
    spread[...] = jnp.where((r == (c // 16) * 15 + c % 16) & (c % 16 != 15), 1.0, 0.0).astype(BF)

    xs[:, 896:1024] = jnp.zeros((ROWS, 128), F32)
    xs[:, 0:D] = x_ref[...].astype(F32)
    go[:, 896:1024] = jnp.zeros((ROWS, 128), BF)
    live = live_ref[:, 0:1]
    go[:, 0:D] = (c_ref[...].astype(F32) * live).astype(BF)
    x = xs[...]
    inv1 = lax.rsqrt(mean_of(x * x) + EPSILON)
    loads[0].wait()
    gains = w[0, 39].astype(F32)
    gain1 = side([gains[i : i + 1] for i in range(8)])
    gain2 = side([gains[8 + i : 9 + i] for i in range(8)])
    nrm[...] = (x * inv1 * gain1).astype(BF)

    cos_t, sin_t = cos_ref[...], sin_ref[...]
    for c in range(0, 13, 2):
        group = [qkv_tiles(i) for i in range(c, min(c + 2, 13))]
        y2 = dot(nrm[:, 0:D], side(group))
        for i in range(len(group)):
            y = y2[:, 128 * i : 128 * i + 128]
            if c + i < 10:
                y = y * cos_t + swap(y) * sin_t
            if c + i < 8:
                qs[c + i] = y.astype(BF)
            for h in range(2):
                head = 2 * (c + i) + h
                if 15 <= head < 20:
                    kk[head - 15] = both(y, h).astype(BF)
                if 20 <= head < 25:
                    vv[head - 20] = both(y, h).astype(BF)

    mixed[:, 896:1024] = jnp.zeros((ROWS, 128), BF)
    zero_b = jnp.zeros((MROWS, 128), BF)

    def rows_of(m):
        return pl.ds(pl.multiple_of(m * MROWS, MROWS), MROWS)

    def chunk(head):
        return pl.ds(128 * (head // 2), 128)

    def attend(m, _):
        rows = rows_of(m)
        bias = bias_ref[rows, :]
        bias3 = jnp.concatenate([bias, bias, bias], axis=0)
        for g in range(KV):
            heads = [3 * g + i for i in range(3)]
            q = jnp.concatenate([jnp.where(half[h % 2], qs[h // 2, rows, :], zero_b) for h in heads], axis=0)
            s = dot(q, kk[g, rows, :], 1, 1) * 0.125 + bias3
            e = jnp.exp(s - jnp.max(s, axis=-1, keepdims=True))
            p = e / jnp.sum(e, axis=-1, keepdims=True)
            prob[m, g] = p
            o = dot(p.astype(BF), vv[g, rows, :]).astype(BF)
            for i, h in enumerate(heads):
                mixed[rows, chunk(h)] = jnp.where(half[h % 2], o[MROWS * i : MROWS * i + MROWS], mixed[rows, chunk(h)])
        return 0

    lax.fori_loop(0, MB, attend, 0)

    loads[1].wait()
    for c in range(0, 8, 2):
        cols = slice(128 * c, 128 * c + 256)
        mid[:, cols] = xs[:, cols] + dot(mixed[:, 0:D], side([out_tiles(c), out_tiles(c + 1)]))
    middle = mid[...]
    inv2 = lax.rsqrt(mean_of(middle * middle) + EPSILON)
    n2p[...] = dot((middle * inv2 * gain2).astype(BF), spread[...]).astype(BF)

    loads[2].wait()

    def expand(c, _):
        g = dot(n2p[...], in_tiles(c))
        u = dot(n2p[...], in_tiles(c + 4))
        gate[c] = g
        up[c] = u
        hid[c] = (g * jax.nn.sigmoid(g) * u).astype(BF)
        return 0

    lax.fori_loop(0, 4, expand, 0)
    loads[3].wait()
    acc[...] = mid[...]

    def reduce_(c, _):
        tiles = down_tiles(c)
        acc[...] += dot(hid[c], tiles)
        gh = dot(go[...], tiles, 1, 1)
        g, u = gate[c], up[c]
        sg = jax.nn.sigmoid(g)
        ggu[c] = (gh * u * sg * (1.0 + g * (1.0 - sg))).astype(BF)
        ggu[c + 4] = (gh * g * sg).astype(BF)
        term = dot(hid[c], go[...], 0, 0).astype(BF)
        for i in range(8):
            w[pl.ds(96 + 8 * c, 8), 5 * i : 5 * i + 5] = term[:, 128 * i : 128 * i + 128].reshape(8, 5, 16, 128)
        return 0

    lax.fori_loop(0, 4, reduce_, 0)
    stores[3].start()
    out_ref[...] = (acc[:, 0:D] * live).astype(BF)

    acc[...] = jnp.zeros((ROWS, 1024), F32)

    def back(c, _):
        gg = ggu[c]
        acc[...] += dot(gg, in_tiles(c), 1, 1)
        term = dot(n2p[...], gg, 0, 0).astype(BF)
        for i in range(5):
            w[32:96, 5 * c + i] = term[:, 128 * i : 128 * i + 128].reshape(64, 16, 128)
        return 0

    lax.fori_loop(0, 8, back, 0)
    stores[2].start()
    gn = acc[...]
    hi = gn.astype(BF)
    lo = (gn - hi.astype(F32)).astype(BF)
    gn = dot(hi, spread[...], 1, 1) + dot(lo, spread[...], 1, 1)
    n2 = mid[...] * inv2
    d_gain2 = jnp.sum(gn * n2, axis=0, keepdims=True)
    u = gn * gain2
    gm = go[...].astype(F32) + inv2 * (u - n2 * mean_of(u * n2))
    mid[...] = gm
    gmb = gm.astype(BF)
    gmix = jnp.zeros((ROWS, D), F32)
    for i in range(0, 8, 2):
        gmix = gmix + dot(gmb[:, 128 * i : 128 * i + 256], side([out_tiles(i), out_tiles(i + 1)]), 1, 1)
    term = dot(mixed[:, 0:D], gmb, 0, 0).astype(BF)
    for i in range(8):
        w[20:32, 5 * i : 5 * i + 5] = term[:, 128 * i : 128 * i + 128].reshape(12, 5, 16, 128)
    stores[1].start()
    mixed[:, 0:D] = gmix.astype(BF)
    gq[12] = jnp.zeros((ROWS, 128), F32)

    def attend_back(m, _):
        rows = rows_of(m)
        for g in range(KV):
            heads = [3 * g + i for i in range(3)]
            q = jnp.concatenate([jnp.where(half[h % 2], qs[h // 2, rows, :], zero_b) for h in heads], axis=0)
            gmx = jnp.concatenate([jnp.where(half[h % 2], mixed[rows, chunk(h)], zero_b) for h in heads], axis=0)
            p = prob[m, g]
            gv = dot(p.astype(BF), gmx, 0, 0)
            gp = dot(gmx, vv[g, rows, :], 1, 1)
            gs = (p * (gp - jnp.sum(p * gp, axis=-1, keepdims=True))).astype(BF)
            gqs = dot(gs, kk[g, rows, :]) * 0.125
            gk = dot(gs, q, 0, 0) * 0.125
            for i, h in enumerate(heads):
                gq[h // 2, rows, :] = jnp.where(half[h % 2], gqs[MROWS * i : MROWS * i + MROWS], gq[h // 2, rows, :])
            for head, value in ((15 + g, gk), (20 + g, gv)):
                value = value + pltpu.roll(value, 64, 1)
                gq[head // 2, rows, :] = jnp.where(half[head % 2], value, gq[head // 2, rows, :])
        return 0

    lax.fori_loop(0, MB, attend_back, 0)

    for c in range(13):
        y = gq[c]
        if c < 10:
            y = y * cos_t - swap(y) * sin_t
        gqb[c] = y.astype(BF)
    gn1 = jnp.zeros((ROWS, D), F32)
    for c in range(0, 13, 2):
        group = list(range(c, min(c + 2, 13)))
        gy = side([gqb[i] for i in group])
        gn1 = gn1 + dot(gy, side([qkv_tiles(i) for i in group]), 1, 1)
        term = dot(nrm[:, 0:D], gy, 0, 0).astype(BF)
        for n, i in enumerate(group):
            w[0:20, 3 * i : 3 * i + 3] = term[:, 128 * n : 128 * n + 128].reshape(20, 3, 16, 128)
    acc[:, 896:1024] = jnp.zeros((ROWS, 128), F32)
    acc[:, 0:D] = gn1
    gn1 = acc[...]
    n1 = xs[...] * inv1
    d_gain1 = jnp.sum(gn1 * n1, axis=0, keepdims=True)
    both_gains = jnp.concatenate([v[:, 128 * i : 128 * i + 128] for v in (d_gain1, d_gain2) for i in range(8)], axis=0)
    w[0, 39] = both_gains.astype(BF)
    stores[0].start()
    u = gn1 * gain1
    res = mid[...] + inv1 * (u - n1 * mean_of(u * n1))
    gin_ref[...] = res[:, 0:D].astype(BF)
    for store in stores:
        store.wait()


def compute(blocks, inputs, cotangent, segments, counts):
    vm = pl.BlockSpec(memory_space=pltpu.VMEM)
    hbm = pl.BlockSpec(memory_space=pl.ANY)
    return pl.pallas_call(
        compute_kernel,
        out_shape=(
            jax.ShapeDtypeStruct((ROWS, D), BF),
            jax.ShapeDtypeStruct((ROWS, D), BF),
            jax.ShapeDtypeStruct((N, 40, 16, 128), BF),
        ),
        in_specs=[hbm] + [vm] * 6,
        out_specs=(vm, vm, hbm),
        scratch_shapes=[
            pltpu.VMEM((N, 40, 16, 128), BF),
            pltpu.VMEM((ROWS, 1024), F32),
            pltpu.VMEM((ROWS, 1024), BF),
            pltpu.VMEM((ROWS, 1024), BF),
            pltpu.VMEM((8, ROWS, 128), BF),
            pltpu.VMEM((KV, ROWS, 128), BF),
            pltpu.VMEM((KV, ROWS, 128), BF),
            pltpu.VMEM((MB, KV, ROWS, MROWS), F32),
            pltpu.VMEM((ROWS, 1024), BF),
            pltpu.VMEM((ROWS, 1024), F32),
            pltpu.VMEM((ROWS, 1024), BF),
            pltpu.VMEM((4, ROWS, 640), F32),
            pltpu.VMEM((4, ROWS, 640), F32),
            pltpu.VMEM((4, ROWS, 640), BF),
            pltpu.VMEM((8, ROWS, 640), BF),
            pltpu.VMEM((13, ROWS, 128), F32),
            pltpu.VMEM((13, ROWS, 128), BF),
            pltpu.VMEM((1024, 1024), BF),
            pltpu.VMEM((ROWS, 1024), F32),
            pltpu.SemaphoreType.DMA((4,)),
            pltpu.SemaphoreType.DMA((4,)),
        ],
        compiler_params=pltpu.CompilerParams(vmem_limit_bytes=60 * 1024 * 1024),
    )(blocks.reshape(N, 40, 16, 128), inputs, cotangent, *tables(segments, counts))


def shards(inputs, cotangent, flat_weights, counts, segments):
    d = lax.axis_index("fsdp")
    blocks = gather(to_block(flat_weights, d))
    block_out, input_grad, terms = compute(blocks, inputs, cotangent, segments, counts)
    return block_out, input_grad, from_block(scatter(terms.reshape(4, 4, 4, 2, TILES, 16, 128)), d)


def solution(mesh):
    in_specs = (P("fsdp", None), P("fsdp", None), P("fsdp"), P("fsdp"), P("fsdp"))
    out_specs = (P("fsdp", None), P("fsdp", None), P("fsdp"))
    return jax.shard_map(shards, mesh=mesh, in_specs=in_specs, out_specs=out_specs, check_vma=False)
```

profile of v0, /device:TPU:0, one launch (start us, length us, event | category | flops | bytes accessed | tf_op | source)
XLA Modules:
  0.0 188.1 jit_solution(13536273709582390106)
XLA Ops:
  0.6 0.7 slice.25
  1.3 8.2 %collective-permute-start = (bf16[1920]{0:T(1024)(128)(2,1)S(1)}, bf16[1920]{0:T(1024)(128)(2,1)S(1)}, u32[]{:S(2)}, u32[]{:S(2)}) collective-permute-start(bf16[1920]{0:T(1024)(128)(2,1)S(1)} %slice.25), channel_id=1, source_target_pairs={{0,127},{1,0},{2,1},{3,2},{4,3},{5,4},{6,5},{7,6},{8,7},{9,8},{10,... | collective-permute-start | bytes 11528 | tf_op jit(solution)/shard_map/ppermute | solution.py:368
  9.5 0.1 reshape.136
  9.6 0.8 eq.27
  10.4 0.2 select_reduce_fusion
  10.6 0.1 convert_element_type.29
  10.7 0.7 fusion.7
  11.5 0.5 fusion.6
  12.0 1.0 pad_maximum_fusion
  13.0 0.1 reshape.152
  13.1 1.4 fusion.5.bias_ref
  14.5 1.4 fusion.3
  15.9 0.2 reshape.133
  16.0 0.1 reshape.137
  16.2 0.2 reshape.139
  16.4 0.1 reshape.134
  16.7 0.8 fusion.2.blk
  17.4 56.9 %shard_map.76 = bf16[4,4,4,2,40,16,128]{6,5,4,3,2,1,0:T(8,128)(2,1)} custom-call(bf16[40,16,128]{2,1,0:T(8,128)(2,1)} %fusion.2.blk), custom_call_target="tpu_custom_call" | custom-call | tf_op jit(solution)/shard_map/pallas_call | solution.py:164
  74.3 0.7 broadcast_in_dim.41.live_ref
  75.1 41.2 %shard_map.77 = (bf16[240,960]{1,0:T(8,128)(2,1)}, bf16[240,960]{1,0:T(8,128)(2,1)}, bf16[128,40,16,128]{3,2,1,0:T(8,128)(2,1)}) custom-call(bf16[128,40,16,128]{3,2,1,0:T(8,128)(2,1)} %bitcast.57, bf16[240,960]{1,0:T(8,128)(2,1)} %x_ref.1, bf16[240,960]{1,0:T(8,128)(2,1)} %c_ref.1, f32[240,128]{1,0:T(8,128)} %get-tuple-element.12.cos_ref, ...), custom_call_target="tpu_custom_call" | custom-call | tf_op jit(solution)/shard_map/pallas_call | solution.py:640
  116.3 58.5 %shard_map.78 = f32[40,16,128]{2,1,0:T(8,128)} custom-call(bf16[4,4,4,2,40,16,128]{6,5,4,3,2,1,0:T(8,128)(2,1)} %bitcast.58), custom_call_target="tpu_custom_call" | custom-call | tf_op jit(solution)/shard_map/pallas_call | solution.py:338
  174.7 1.0 slice.28
  175.7 1.1 copy.19
  176.8 0.1 copy.18
  176.9 0.1 copy.29
  177.0 0.2 reshape.147
  177.2 1.1 copy.20
  178.4 0.2 reshape.151
  178.6 0.1 select_select_fusion
  178.7 0.7 slice.26
  179.5 7.7 %collective-permute-done.1 = f32[1920]{0:T(1024)S(1)} collective-permute-done((f32[1920]{0:T(1024)S(1)}, f32[1920]{0:T(1024)S(1)}, u32[]{:S(2)}, u32[]{:S(2)}) %collective-permute-start.1) | collective-permute-done | bytes 7712 | tf_op jit(solution)/shard_map/ppermute | solution.py:379
  187.2 0.9 fusion
  (18 shorter events, 0.4 us)
Async XLA Ops:
  1.3 13.2 %collective-permute-start = (bf16[1920]{0:T(1024)(128)(2,1)S(1)}, bf16[1920]{0:T(1024)(128)(2,1)S(1)}, u32[]{:S(2)}, u32[]{:S(2)}) collective-permute-start(bf16[1920]{0:T(1024)(128)(2,1)S(1)} %slice.25), channel_id=1, source_target_pairs={{0,127},{1,0},{2,1},{3,2},{4,3},{5,4},{6,5},{7,6},{8,7},{9,8},{10,... | collective-permute-start | bytes 11528 | tf_op jit(solution)/shard_map/ppermute | solution.py:368
  178.7 8.6 %collective-permute-start.1 = (f32[1920]{0:T(1024)S(1)}, f32[1920]{0:T(1024)S(1)}, u32[]{:S(2)}, u32[]{:S(2)}) collective-permute-start(f32[1920]{0:T(1024)S(1)} %slice.37), channel_id=1, source_target_pairs={{0,1},{1,2},{2,3},{3,4},{4,5},{5,6},{6,7},{7,8},{8,9},{9,10},{10,1... | collective-permute-start | bytes 23048 | tf_op jit(solution)/shard_map/ppermute | solution.py:379
where the time goes:
time: 189 us; the launch traced here: 188 us
  Pallas kernels  157 us (83%)
  starting transfers between devices  8.28 us (4%)
  local copies, waits for them, and re-layouts  7.78 us (4%)
  waiting for transfers between devices  7.7 us (4%)
  other arithmetic  6.99 us (4%)
    pallas_call x1, Pallas kernels, scatter(): pl.pallas_call(scatter_kernel, out_shape=jax.ShapeDtypeStruct((TILES, 16,...  58.5 us
    pallas_call x1, Pallas kernels, gather(): pl.pallas_call(gather_kernel, out_shape=jax.ShapeDtypeStruct((4, 4, 4, 2,...  56.9 us
    pallas_call x1, Pallas kernels, compute(): pl.pallas_call(compute_kernel, out_shape=(jax.ShapeDtypeStruct((ROWS, D),...  41.2 us
    ppermute x1, starting transfers between devices, to_block(): lax.ppermute(shard[:GAINS], 'fsdp', [(i, (i + N - 1) % N) for i in range(...  8.21 us
    ppermute x1, waiting for transfers between devices, from_block(): lax.ppermute(flat[BLOCK - GAINS:], 'fsdp', [(i, (i + 1) % N) for i in ran...  7.7 us
  transfers between devices with their start and end apart: 2, of which 1 were waited for; matrix products, arithmetic and copies ran while one was open for 3% of the time, Pallas kernels for 0%

commit v1 on v0

v1 whole, which is shorter than its diff:
```python
import functools
import math

import jax
import jax.numpy as jnp
from jax import lax
from jax.experimental import pallas as pl
from jax.experimental.pallas import tpu as pltpu
from jax.sharding import PartitionSpec as P

D = 960
H = 15
KV = 5
HD = 64
FF = 2560
MB = 3
EPSILON = 1e-05
GAINS = 2 * D
BLOCK = 76800
N = 128
BF = jnp.bfloat16
F32 = jnp.float32
VMEM_BYTES = 63 * 1024 * 1024

MESH = pl.DeviceIdType.MESH
TILES = 40
PARTS = ((0, 7, 14), (14, 20, 27), (27, 33, 40))


def place():
    me = lax.axis_index("fsdp")
    return [me // 32, (me // 8) % 4, (me // 2) % 4], me % 2


def device_at(coords, core):
    return (coords[0] * 32 + coords[1] * 8 + coords[2] * 2 + core,)


def moved(coords, dim, by):
    out = list(coords)
    out[dim] = (out[dim] + by + 4) % 4
    return out


def greet(coords, core):
    barrier = pltpu.get_barrier_semaphore()
    for dim in range(3):
        for by in (1, -1, 2):
            pl.semaphore_signal(barrier, inc=1, device_id=device_at(moved(coords, dim, by), core), device_id_type=MESH)
    pl.semaphore_signal(barrier, inc=1, device_id=device_at(coords, 1 - core), device_id_type=MESH)
    pl.semaphore_wait(barrier, 10)


def gather_into(w, blk, coords, core, send, recv, pair_send, pair_recv, own_sem):
    sent, ids, pair_ids, swapped = [], {}, {}, []
    sibling = device_at(coords, 1 - core)

    def at(fixed, tiles, which):
        index = [slice(None)] * 3
        for dim, value in fixed.items():
            index[dim] = value
        return w.at[(*index, which, rng(tiles))]

    def push(src, dst, device, ssem, rsem):
        copy = pltpu.make_async_remote_copy(src_ref=src, dst_ref=dst, send_sem=ssem, recv_sem=rsem, device_id=device, device_id_type=MESH)
        copy.start()
        sent.append(copy)

    def forward(key, src, dst, dim, step):
        k = ids.setdefault(key, len(ids))
        push(src, dst, device_at(moved(coords, dim, step), core), send.at[k], recv.at[k])

    def arrived(key, ref):
        landed(ref, recv.at[ids[key]])

    def swap(fixed, tiles):
        k = len(swapped)
        push(at(fixed, tiles, core), at(fixed, tiles, core), sibling, pair_send.at[k], pair_recv.at[k])
        swapped.append((fixed, tiles, k))

    def half(p, sign, number):
        lo, mid, hi = PARTS[p]
        return ((lo, mid), (mid, hi))[(number == 1) ^ (sign < 0)]

    def whole(p):
        return (PARTS[p][0], PARTS[p][2])

    def near(dim, step):
        return moved(coords, dim, step)[dim]

    local = pltpu.make_async_copy(blk, w.at[(*coords, core)], own_sem)
    local.start()
    parts = range(3)
    dims = [[(p + k) % 3 for k in range(3)] for p in parts]
    for p in parts:
        a, b, c = dims[p]
        for step in (2, 1, -1):
            forward((p, 0, step), blk.at[rng(whole(p))], at({a: coords[a], b: coords[b], c: coords[c]}, whole(p), core), a, step)
    push(blk, w.at[(*coords, core)], sibling, pair_send.at[90], pair_recv.at[90])
    local.wait()

    def line(p, step):
        a, b, c = dims[p]
        return {b: near(b, step), c: coords[c]}

    def sheet(p, group, step):
        a, b, c = dims[p]
        return {b: near(b, group), c: near(c, step)}

    def send_line(p, number):
        for sign in (1, -1):
            ref = at(line(p, 0), half(p, sign, number), core)
            forward((p, 1, sign, number), ref, ref, dims[p][1], sign)

    def send_sheet(p, group, number):
        for sign in (1, -1):
            ref = at(sheet(p, group, 0), half(p, sign, number), core)
            forward((p, 2, group, sign, number), ref, ref, dims[p][2], sign)

    def relay_line(p):
        for sign in (1, -1):
            ref = at(line(p, -sign), half(p, sign, 0), core)
            arrived((p, 1, sign, 0), ref)
            forward((p, 1, sign, 2), ref, ref, dims[p][1], sign)

    def relay_sheet(p, group):
        for sign in (1, -1):
            ref = at(sheet(p, group, -sign), half(p, sign, 0), core)
            arrived((p, 2, group, sign, 0), ref)
            forward((p, 2, group, sign, 2), ref, ref, dims[p][2], sign)

    def rest_sheet(p, group):
        for sign in (1, -1):
            arrived((p, 2, group, sign, 1), at(sheet(p, group, -sign), half(p, sign, 1), core))
            swap(sheet(p, group, -sign), whole(p))

    def last_sheet(p, group):
        for sign in (1, -1):
            arrived((p, 2, group, sign, 2), at(sheet(p, group, 2), half(p, sign, 2), core))
        swap(sheet(p, group, 2), whole(p))

    for p in parts:
        a, b, c = dims[p]
        for step in (1, -1, 2):
            fixed = {a: near(a, -step), b: coords[b], c: coords[c]}
            arrived((p, 0, step), at(fixed, whole(p), core))
            swap(fixed, whole(p))
        for number in (0, 1):
            send_line(p, number)
    for p in parts:
        for number in (0, 1):
            send_sheet(p, 0, number)
    for p in parts:
        relay_line(p)
    for p in parts:
        for sign in (1, -1):
            arrived((p, 1, sign, 1), at(line(p, -sign), half(p, sign, 1), core))
        for sign in (1, -1):
            for number in (0, 1):
                send_sheet(p, -sign, number)
    for p in parts:
        relay_sheet(p, 0)
    for p in parts:
        for sign in (1, -1):
            arrived((p, 1, sign, 2), at(line(p, 2), half(p, sign, 2), core))
        for number in (0, 1):
            send_sheet(p, 2, number)
        for step in (1, -1, 2):
            swap(line(p, step), whole(p))
    for p in parts:
        rest_sheet(p, 0)
    for group in (-1, 1, 2):
        for p in parts:
            relay_sheet(p, group)
        for p in parts:
            rest_sheet(p, group)
    for group in (0, -1, 1, 2):
        for p in parts:
            last_sheet(p, group)
    landed(w.at[(*coords, 1 - core)], pair_recv.at[90])
    for fixed, tiles, k in swapped:
        landed(at(fixed, tiles, 1 - core), pair_recv.at[k])
    return sent


def pack(rows_48, rows_80, rows_15, gains, d):
    qkv = jnp.pad(rows_48, ((0, 0), (0, 64))).reshape(3, 16, 13, 128).transpose(2, 0, 1, 3).reshape(39, 16, 128)
    qkv = jnp.concatenate([qkv, jnp.where(d == 0, gains, jnp.zeros_like(gains))[None]], axis=0)
    square = jnp.pad(rows_80, ((0, 0), (0, 64))).reshape(5, 16, 8, 128).transpose(2, 0, 1, 3).reshape(40, 16, 128)
    wide = jnp.pad(rows_15, ((0, 1), (0, 0))).reshape(16, 40, 128).transpose(1, 0, 2)
    return jnp.where(d < 20, qkv, jnp.where((d >= 32) & (d < 96), wide, square))


def to_block(shard, d):
    following = lax.ppermute(shard[:GAINS], "fsdp", [(i, (i + N - 1) % N) for i in range(N)])
    flat = lax.dynamic_slice(jnp.concatenate([shard, following]), (GAINS - 15 * d,), (BLOCK,))
    gains = jnp.pad(shard[:GAINS].reshape(2, D), ((0, 0), (0, 64))).reshape(16, 128)
    return pack(flat.reshape(48, 1600), flat.reshape(80, D), flat.reshape(15, 2 * FF), gains, d)


def from_block(tiles, d):
    qkv = tiles[:39].reshape(13, 3, 16, 128).transpose(1, 2, 0, 3).reshape(48, 1664)[:, :1600].reshape(-1)
    square = tiles.reshape(8, 5, 16, 128).transpose(1, 2, 0, 3).reshape(80, 1024)[:, :D].reshape(-1)
    wide = tiles.transpose(1, 0, 2)[:15].reshape(-1)
    flat = jnp.where(d < 20, qkv, jnp.where((d >= 32) & (d < 96), wide, square))
    before = lax.ppermute(flat[BLOCK - GAINS :], "fsdp", [(i, (i + 1) % N) for i in range(N)])
    before = jnp.where(d == 0, tiles[39].reshape(2, 1024)[:, :D].reshape(-1), before)
    return lax.dynamic_slice(jnp.concatenate([before, flat]), (15 * d,), (BLOCK + 15,))


ROWS = 240
MROWS = 80


def tables(segment_ids, counts):
    seg = segment_ids.reshape(MB, MROWS)
    places = jnp.arange(MROWS, dtype=jnp.int32)
    same = seg[:, :, None] == seg[:, None, :]
    first_row = jnp.min(jnp.where(same, places[None, None, :], MROWS), axis=2)
    position = (places[None, :] - first_row).astype(F32).reshape(ROWS)
    freq = jnp.exp(jnp.arange(HD // 2, dtype=F32) * (-2.0 * math.log(10000.0) / HD))
    angle = position[:, None] * freq[None, :]
    cos, sin = jnp.cos(angle), jnp.sin(angle)
    cos_t = jnp.concatenate([cos, cos, cos, cos], axis=1)
    sin_t = jnp.concatenate([-sin, sin, -sin, sin], axis=1)
    allowed = same & (places[None, None, :] <= places[None, :, None])
    bias = jnp.where(allowed, 0.0, -1e30).astype(F32).reshape(ROWS, MROWS)
    live = (places[None, :] < counts[:, None]).astype(F32).reshape(ROWS, 1)
    return cos_t, sin_t, bias, jnp.broadcast_to(live, (ROWS, 128))


def dot(a, b, ca=1, cb=0):
    return lax.dot_general(a, b, (((ca,), (cb,)), ((), ())), preferred_element_type=F32)


def mean_of(value):
    return jnp.sum(value, axis=-1, keepdims=True) * (1.0 / D)


class Flow:
    def __init__(self, name, dims, tiles, bufs, first_plane):
        self.name, self.dims, self.tiles, self.bufs, self.first_plane = name, dims, tiles, bufs, first_plane

    def half(self, sign, which):
        lo, mid, hi = self.tiles
        pair = ((lo, mid), (mid, hi))
        return pair[which] if sign > 0 else pair[1 - which]


class Reduce:
    def __init__(self, w, pair_buf, bufs, red, coords, core, send, recv, pair_send, pair_recv):
        self.w, self.pair_buf, self.red = w, pair_buf, red
        self.coords, self.core = coords, core
        self.send, self.recv, self.pair_send, self.pair_recv = send, recv, pair_send, pair_recv
        self.sent, self.ids = [], {}
        b1, b2, b3, q1, q2, z2 = bufs
        self.P0 = Flow("P0", (0, 1, 2), (0, 5, 10), (b1, b2, b3), 0)
        self.P1 = Flow("P1", (1, 2, 0), (10, 17, 25), (b1, b2, None), 0)
        self.P2 = Flow("P2", (2, 1, 0), (25, 32, 40), (b1, b2, None), 0)
        self.Q1 = Flow("Q1", (1, 2, 0), (0, 10, 20), (q1, q2, None), 0)
        self.Q2 = Flow("Q2", (2, 1, 0), (20, 30, 40), (q1, q2, None), 0)
        self.Z1 = Flow("Z1", (1, 2, 0), (10, 25, 40), (None, None, b3), 0)
        self.Z2 = Flow("Z2", (1, 2, 0), (0, 5, 10), (None, None, z2), 0)

    def copy(self, src, dst, device, ssem, rsem):
        return pltpu.make_async_remote_copy(
            src_ref=src, dst_ref=dst, send_sem=ssem, recv_sem=rsem, device_id=device, device_id_type=MESH
        )

    def offer(self, z):
        one = self.copy(
            self.w.at[z, :, :, 1 - self.core], self.pair_buf.at[z % 3], device_at(self.coords, 1 - self.core),
            self.pair_send.at[z], self.pair_recv.at[z],
        )
        one.start()
        self.sent.append((None, one))

    def ready(self, z):
        slot = z % 3
        landed(self.pair_buf.at[slot], self.pair_recv.at[z])

        def body(t, _):
            at = (z, t // 4, t % 4, self.core)
            self.w[at] = self.w[at] + self.pair_buf[slot, t // 4, t % 4]
            return 0

        lax.fori_loop(0, 16, body, 0)

    def sem(self, flow, phase, planes, sign, number):
        return self.ids.setdefault((flow.name, phase, planes, sign, number), len(self.ids))

    def along(self, dim, step):
        return moved(self.coords, dim, step)[dim]

    def slot(self, flow, phase, planes, sign, number):
        which = 2 if number == 0 else (0 if sign > 0 else 1)
        inner = []
        for d in range(3):
            if d in flow.dims[phase + 1 :]:
                inner.append(pl.ds(planes[0], planes[1] - planes[0]) if d == 0 else slice(None))
        if flow.name in ("Q1", "Q2"):
            inner = inner[1:]
        tiles = flow.half(sign, 1 if number == 1 else 0)
        return flow.bufs[phase].at[(which, *inner, rng(tiles))]

    def ship(self, flow, phase, planes, sign, number):
        dim = flow.dims[phase]
        tiles = flow.half(sign, 1 if number == 1 else 0)
        fixed = []
        for d in range(3):
            if d in flow.dims[:phase]:
                fixed.append(self.coords[d])
            elif d == dim:
                fixed.append(self.along(d, 2 if number == 0 else sign))
            else:
                fixed.append(pl.ds(planes[0], planes[1] - planes[0]) if d == 0 else slice(None))
        slot = self.slot(flow, phase, planes, sign, number)
        if flow.name in ("Q1", "Q2"):
            fixed[0] = 0
        k = self.sem(flow, phase, planes, sign, number)
        return self.copy(
            self.w.at[(*fixed, self.core, rng(tiles))], slot,
            device_at(moved(self.coords, dim, sign), self.core), self.send.at[k], self.recv.at[k],
        )

    def go(self, flow, phase, planes, sign, number, guard=None):
        one = self.ship(flow, phase, planes, sign, number)
        if guard is None:
            one.start()
        else:
            pl.when(guard)(one.start)
        self.sent.append((guard, one))

    def loop(self, flow, phase, planes, coord, fn):
        dims = flow.dims
        free = [d for d in range(3) if d in dims[phase + 1 :]]
        sizes = [planes[1] - planes[0] if d == 0 else 4 for d in free]

        def body(t, _):
            inner = []
            if len(free) == 2:
                inner = [t // 4 + (planes[0] if free[0] == 0 else 0), t % 4]
            elif len(free) == 1:
                inner = [t + (planes[0] if free[0] == 0 else 0)]
            at = []
            for d in range(3):
                if d in free:
                    at.append(inner[free.index(d)])
                elif d == dims[phase]:
                    at.append(coord)
                else:
                    at.append(self.coords[d])
            if flow.name in ("Q1", "Q2"):
                at[0] = 0
                inner = inner[1:]
            fn((*at, self.core), tuple(inner))
            return 0

        count = math.prod(sizes)
        if count == 1:
            body(0, 0)
        else:
            lax.fori_loop(0, count, body, 0)

    def add_half(self, flow, phase, planes, sign):
        landed(self.slot(flow, phase, planes, sign, 0), self.recv.at[self.sem(flow, phase, planes, sign, 0)])
        tiles = rng(flow.half(sign, 0))
        buf = flow.bufs[phase]

        def fold(at, inner):
            self.w[(*at, tiles)] = self.w[(*at, tiles)] + buf[(2, *inner, tiles)]

        self.loop(flow, phase, planes, self.along(flow.dims[phase], sign), fold)

    def add_all(self, flow, phase, planes):
        for sign in (1, -1):
            for number in (1, 2):
                landed(self.slot(flow, phase, planes, sign, number), self.recv.at[self.sem(flow, phase, planes, sign, number)])
        tiles = rng((flow.tiles[0], flow.tiles[2]))
        buf = flow.bufs[phase]

        def total(at, inner):
            value = self.w[(*at, tiles)].astype(F32) + buf[(0, *inner, tiles)].astype(F32) + buf[(1, *inner, tiles)].astype(F32)
            if phase == 2:
                self.red[tiles] = value
            else:
                self.w[(*at, tiles)] = value.astype(BF)

        self.loop(flow, phase, planes, self.coords[flow.dims[phase]], total)

    def plane_in(self, planes, step):
        z = self.along(0, step)
        return (z >= planes[0]) & (z < planes[1])

    def first(self, planes):
        for z in range(*planes):
            self.ready(z)
        flows = (self.P1, self.P2) if planes[0] else (self.Q1, self.Q2)
        for number in (0, 1):
            for sign in (1, -1):
                for flow in flows:
                    self.go(flow, 0, planes, sign, number)
                if planes[0]:
                    one = self.ship(self.P0, 0, (0, 4), sign, number)
                    pl.when(self.plane_in(planes, 2 if number == 0 else sign))(one.start)

    def second(self, planes):
        for sign in (1, -1):
            if planes[0]:

                @pl.when(self.plane_in(planes, sign))
                def _():
                    self.add_half(self.P0, 0, (0, 4), sign)
                    self.ship(self.P0, 0, (0, 4), sign, 2).start()

            for flow in (self.P1, self.P2) if planes[0] else (self.Q1, self.Q2):
                self.add_half(flow, 0, planes, sign)
                self.go(flow, 0, planes, sign, 2)

    def start(self, flow, phase, planes, guards=None):
        for number in (0, 1):
            for sign in (1, -1):
                self.go(flow, phase, planes, sign, number, guards and guards(sign, number))

    def pass_on(self, flow, phase, planes, guards=None):
        for sign in (1, -1):
            guard = guards and guards(sign, 2)
            if guard is None:
                self.add_half(flow, phase, planes, sign)
            else:
                pl.when(guard)(functools.partial(self.add_half, flow, phase, planes, sign))
            self.go(flow, phase, planes, sign, 2, guard)

    def whole(self, flow):
        return rng((flow.tiles[0], flow.tiles[2]))

    def direct(self, flow, phase, planes, step):
        dim = flow.dims[phase]
        fixed, inner = [], []
        for d in range(3):
            if d in flow.dims[:phase]:
                fixed.append(self.coords[d])
            elif d == dim:
                fixed.append(self.along(d, step))
            else:
                span = pl.ds(planes[0], planes[1] - planes[0]) if d == 0 else slice(None)
                fixed.append(span)
                inner.append(span)
        if flow.name in ("Q1", "Q2"):
            fixed[0] = 0
            inner = inner[1:]
        k = self.sem(flow, phase, planes, step, 3)
        return self.copy(
            self.w.at[(*fixed, self.core, self.whole(flow))], flow.bufs[phase].at[(step % 4 - 1, *inner, self.whole(flow))],
            device_at(moved(self.coords, dim, step), self.core), self.send.at[k], self.recv.at[k],
        )

    def start_direct(self, flow, phase, planes, guards=None):
        for step in (2, 1, -1):
            guard = guards and guards(step)
            one = self.direct(flow, phase, planes, step)
            if guard is None:
                one.start()
            else:
                pl.when(guard)(one.start)
            self.sent.append((guard, one))

    def add_direct(self, flow, phase, planes):
        for step in (1, -1, 2):
            self.direct(flow, phase, planes, step).wait_recv()
        tiles = self.whole(flow)
        buf = flow.bufs[phase]

        def total(at, inner):
            value = self.w[(*at, tiles)].astype(F32)
            for slot in range(3):
                value = value + buf[(slot, *inner, tiles)].astype(F32)
            if phase == 2:
                self.red[tiles] = value
            else:
                self.w[(*at, tiles)] = value.astype(BF)

        self.loop(flow, phase, planes, self.coords[flow.dims[phase]], total)

    def finish(self):
        late, early, every = (0, 1), (1, 4), (0, 4)
        z = self.coords[0]
        upper = lambda sign, number=0: z != 0
        to_zero = lambda step: self.along(0, step) == 0
        for number in (0, 1, 2):
            for sign in (1, -1):
                guard = self.plane_in((1, 4), 2 if number == 0 else sign)
                self.sent.append((guard, self.ship(self.P0, 0, every, sign, number)))
        for flow in (self.P1, self.P2):
            for planes in ((3, 4), (1, 3)):
                self.add_all(flow, 0, planes)
            self.start(flow, 1, early)
        self.second(late)
        pl.when(z != 0)(lambda: self.add_all(self.P0, 0, every))
        self.start(self.P0, 1, every, upper)
        for flow in (self.P1, self.P2):
            self.pass_on(flow, 1, early)
        for flow in (self.Q1, self.Q2):
            self.add_all(flow, 0, late)
            self.start_direct(flow, 1, late)
        self.pass_on(self.P0, 1, every, upper)
        for flow in (self.P1, self.P2):
            self.add_all(flow, 1, early)
        for flow in (self.Q1, self.Q2):
            self.add_direct(flow, 1, late)
        self.start_direct(self.Z1, 2, every)
        self.start_direct(self.Z2, 2, every, to_zero)
        pl.when(z != 0)(lambda: self.add_all(self.P0, 1, every))
        self.start_direct(self.P0, 2, every, upper)
        self.add_direct(self.Z1, 2, every)
        pl.when(z != 0)(lambda: self.add_direct(self.P0, 2, every))
        pl.when(z == 0)(lambda: self.add_direct(self.Z2, 2, every))
        for guard, one in self.sent:
            if guard is None:
                one.wait_send()
            else:
                pl.when(guard)(one.wait_send)


def rng(tiles):
    return pl.ds(tiles[0], tiles[1] - tiles[0])


def landed(dst, rsem):
    pltpu.make_async_copy(dst, dst, rsem).wait()


def layer_kernel(
    blk, x_ref, c_ref, cos_ref, sin_ref, bias_ref, live_ref,
    out_ref, gin_ref, red_ref,
    w, pair_buf, b1, b2, b3, q1, q2, z2, xs, go, nrm, qs, kk, vv, prob, mixed, mid, n2p, gate, up, hid, ggu, gq, gqb, spread, acc,
    send, recv, pair_send, pair_recv, own_sem, rs_send, rs_recv, rp_send, rp_recv,
):
    coords, core = place()
    greet(coords, core)
    sent = gather_into(w, blk, coords, core, send, recv, pair_send, pair_recv, own_sem)
    rs = Reduce(w, pair_buf, (b1, b2, b3, q1, q2, z2), red_ref, coords, core, rs_send, rs_recv, rp_send, rp_recv)

    def join(parts):
        return jnp.concatenate(parts, axis=0)

    def qkv_tiles(c):
        t = slice(3 * c, 3 * c + 3)
        return join([w[0, 0:2, :, :, t].reshape(768, 128), w[0, 2, 0:2, :, t].reshape(192, 128)])

    def put_qkv(c, v):
        t = slice(3 * c, 3 * c + 3)
        w[0, 0:2, :, :, t] = v[:768].reshape(2, 4, 2, 3, 16, 128)
        w[0, 2, 0:2, :, t] = v[768:].reshape(2, 2, 3, 16, 128)

    def out_tiles(c):
        t = slice(5 * c, 5 * c + 5)
        return join([w[0, 2, 2:4, :, t].reshape(320, 128), w[0, 3, :, :, t].reshape(640, 128)])

    def put_out(c, v):
        t = slice(5 * c, 5 * c + 5)
        w[0, 2, 2:4, :, t] = v[:320].reshape(2, 2, 5, 16, 128)
        w[0, 3, :, :, t] = v[320:].reshape(4, 2, 5, 16, 128)

    def in_tiles(c):
        return side([w[1:3, :, :, :, 5 * c + i].reshape(1024, 128) for i in range(5)])

    def down_tiles(c):
        return side([w[3, c, :, :, 5 * i : 5 * i + 5].reshape(640, 128) for i in range(8)])

    def side(parts):
        return jnp.concatenate(parts, axis=1)

    lane = lax.broadcasted_iota(jnp.int32, (MROWS, 128), 1)
    half = (lane < 64, lane >= 64)
    lane_all = lax.broadcasted_iota(jnp.int32, (ROWS, 128), 1)
    low_all = lane_all < 64
    first_all = lane_all % 64 < 32

    def swap(v):
        return jnp.where(first_all, pltpu.roll(v, 96, 1), pltpu.roll(v, 32, 1))

    def both(v, h):
        other = pltpu.roll(v, 64, 1)
        return jnp.where(low_all, v, other) if h == 0 else jnp.where(low_all, other, v)

    for k in range(8):
        r = lax.broadcasted_iota(jnp.int32, (256, 128), 0) + 128 * (k - 1)
        c = lax.broadcasted_iota(jnp.int32, (256, 128), 1) + 128 * k
        spread[k] = jnp.where((r == (c // 16) * 15 + c % 16) & (c % 16 != 15), 1.0, 0.0).astype(BF)

    xs[:, 896:1024] = jnp.zeros((ROWS, 128), BF)
    xs[:, 0:D] = x_ref[...]
    go[:, 896:1024] = jnp.zeros((ROWS, 128), BF)
    live = live_ref[:, 0:1]
    go[:, 0:D] = (c_ref[...].astype(F32) * live).astype(BF)
    x = xs[...].astype(F32)
    inv1 = lax.rsqrt(mean_of(x * x) + EPSILON)
    gains = w[0, 0, 0, 0, 39].astype(F32)
    gain1 = side([gains[i : i + 1] for i in range(8)])
    gain2 = side([gains[8 + i : 9 + i] for i in range(8)])
    nrm[...] = (x * inv1 * gain1).astype(BF)

    cos_t, sin_t = cos_ref[...], sin_ref[...]
    for c in range(0, 13, 2):
        group = [qkv_tiles(i) for i in range(c, min(c + 2, 13))]
        y2 = dot(nrm[:, 0:D], side(group))
        for i in range(len(group)):
            y = y2[:, 128 * i : 128 * i + 128]
            if c + i < 10:
                y = y * cos_t + swap(y) * sin_t
            if c + i < 8:
                qs[c + i] = y.astype(BF)
            for h in range(2):
                head = 2 * (c + i) + h
                if 15 <= head < 20:
                    kk[head - 15] = both(y, h).astype(BF)
                if 20 <= head < 25:
                    vv[head - 20] = both(y, h).astype(BF)

    mixed[:, 896:1024] = jnp.zeros((ROWS, 128), BF)
    zero_b = jnp.zeros((MROWS, 128), BF)

    def rows_of(m):
        return pl.ds(pl.multiple_of(m * MROWS, MROWS), MROWS)

    def chunk(head):
        return pl.ds(128 * (head // 2), 128)

    def attend(m, _):
        rows = rows_of(m)
        bias = bias_ref[rows, :]
        bias3 = jnp.concatenate([bias, bias, bias], axis=0)
        for g in range(KV):
            heads = [3 * g + i for i in range(3)]
            q = jnp.concatenate([jnp.where(half[h % 2], qs[h // 2, rows, :], zero_b) for h in heads], axis=0)
            s = dot(q, kk[g, rows, :], 1, 1) * 0.125 + bias3
            e = jnp.exp(s - jnp.max(s, axis=-1, keepdims=True))
            p = e / jnp.sum(e, axis=-1, keepdims=True)
            prob[m, g] = p
            o = dot(p.astype(BF), vv[g, rows, :]).astype(BF)
            for i, h in enumerate(heads):
                mixed[rows, chunk(h)] = jnp.where(half[h % 2], o[MROWS * i : MROWS * i + MROWS], mixed[rows, chunk(h)])
        return 0

    lax.fori_loop(0, MB, attend, 0)

    for c in range(0, 8, 2):
        cols = slice(128 * c, 128 * c + 256)
        mid[:, cols] = xs[:, cols].astype(F32) + dot(mixed[:, 0:D], side([out_tiles(c), out_tiles(c + 1)]))
    middle = mid[...]
    inv2 = lax.rsqrt(mean_of(middle * middle) + EPSILON)
    n2b = (middle * inv2 * gain2).astype(BF)
    n2p[:, 0:128] = dot(n2b[:, 0:128], spread[0, 128:256]).astype(BF)
    for k in range(1, 8):
        n2p[:, 128 * k : 128 * k + 128] = dot(n2b[:, 128 * k - 128 : 128 * k + 128], spread[k]).astype(BF)


    def expand(c, _):
        g = dot(n2p[...], in_tiles(c))
        u = dot(n2p[...], in_tiles(c + 4))
        gate[c] = g.astype(BF)
        up[c] = u.astype(BF)
        hid[c] = (g * jax.nn.sigmoid(g) * u).astype(BF)
        return 0

    lax.fori_loop(0, 4, expand, 0)
    for copy in sent:
        copy.wait_send()
    acc[...] = mid[...]

    def reduce_(c, _):
        tiles = down_tiles(c)
        acc[...] += dot(hid[c], tiles)
        gh = dot(go[...], tiles, 1, 1)
        g, u = gate[c].astype(F32), up[c].astype(F32)
        sg = jax.nn.sigmoid(g)
        ggu[c] = (gh * u * sg * (1.0 + g * (1.0 - sg))).astype(BF)
        ggu[c + 4] = (gh * g * sg).astype(BF)
        for i in range(0, 8, 2):
            term = dot(hid[c], go[:, 128 * i : 128 * i + 256], 0, 0).astype(BF)
            for n in range(2):
                w[3, c, :, :, 5 * (i + n) : 5 * (i + n) + 5] = term[:, 128 * n : 128 * n + 128].reshape(4, 2, 5, 16, 128)
        return 0

    lax.fori_loop(0, 4, reduce_, 0)
    rs.offer(3)
    out_ref[...] = (acc[:, 0:D] * live).astype(BF)

    acc[...] = jnp.zeros((ROWS, 1024), F32)

    def back(c, _):
        gg = ggu[c]
        acc[...] += dot(gg, in_tiles(c), 1, 1)
        for i in range(0, 5, 2):
            term = dot(n2p[...], gg[:, 128 * i : min(128 * i + 256, 640)], 0, 0).astype(BF)
            for n in range(min(2, 5 - i)):
                w[1:3, :, :, :, 5 * c + i + n] = term[:, 128 * n : 128 * n + 128].reshape(2, 4, 4, 2, 16, 128)
        return 0

    lax.fori_loop(0, 4, back, 0)
    rs.first((3, 4))
    lax.fori_loop(4, 8, back, 0)
    rs.offer(1)
    rs.offer(2)
    rs.second((3, 4))
    gn = acc[...]
    hi = gn.astype(BF)
    lo = (gn - hi.astype(F32)).astype(BF)

    def close(k, part):
        cols = slice(128 * k, 128 * k + 128)
        return dot(hi[:, cols], spread[k, part], 1, 1) + dot(lo[:, cols], spread[k, part], 1, 1)

    before, same = slice(0, 128), slice(128, 256)
    gn = side([close(k, same) + close(k + 1, before) if k < 7 else close(k, same) for k in range(8)])
    n2 = mid[...] * inv2
    d_gain2 = jnp.sum(gn * n2, axis=0, keepdims=True)
    u = gn * gain2
    gm = go[...].astype(F32) + inv2 * (u - n2 * mean_of(u * n2))
    mid[...] = gm
    gmb = gm.astype(BF)
    gmix = jnp.zeros((ROWS, D), F32)
    for i in range(0, 8, 2):
        gmix = gmix + dot(gmb[:, 128 * i : 128 * i + 256], side([out_tiles(i), out_tiles(i + 1)]), 1, 1)
    term = dot(mixed[:, 0:D], gmb, 0, 0).astype(BF)
    for i in range(8):
        put_out(i, term[:, 128 * i : 128 * i + 128])
    rs.first((1, 3))
    mixed[:, 0:D] = gmix.astype(BF)
    gq[12] = jnp.zeros((ROWS, 128), F32)

    def attend_back(m, _):
        rows = rows_of(m)
        for g in range(KV):
            heads = [3 * g + i for i in range(3)]
            q = jnp.concatenate([jnp.where(half[h % 2], qs[h // 2, rows, :], zero_b) for h in heads], axis=0)
            gmx = jnp.concatenate([jnp.where(half[h % 2], mixed[rows, chunk(h)], zero_b) for h in heads], axis=0)
            p = prob[m, g]
            gv = dot(p.astype(BF), gmx, 0, 0)
            gp = dot(gmx, vv[g, rows, :], 1, 1)
            gs = (p * (gp - jnp.sum(p * gp, axis=-1, keepdims=True))).astype(BF)
            gqs = dot(gs, kk[g, rows, :]) * 0.125
            gk = dot(gs, q, 0, 0) * 0.125
            for i, h in enumerate(heads):
                gq[h // 2, rows, :] = jnp.where(half[h % 2], gqs[MROWS * i : MROWS * i + MROWS], gq[h // 2, rows, :])
            for head, value in ((15 + g, gk), (20 + g, gv)):
                value = value + pltpu.roll(value, 64, 1)
                gq[head // 2, rows, :] = jnp.where(half[head % 2], value, gq[head // 2, rows, :])
        return 0

    lax.fori_loop(0, 2, attend_back, 0)
    rs.second((1, 3))
    lax.fori_loop(2, MB, attend_back, 0)

    for c in range(13):
        y = gq[c]
        if c < 10:
            y = y * cos_t - swap(y) * sin_t
        gqb[c] = y.astype(BF)
    gn1 = jnp.zeros((ROWS, D), F32)
    for c in range(0, 13, 2):
        group = list(range(c, min(c + 2, 13)))
        gy = side([gqb[i] for i in group])
        gn1 = gn1 + dot(gy, side([qkv_tiles(i) for i in group]), 1, 1)
        term = dot(nrm[:, 0:D], gy, 0, 0).astype(BF)
        for n, i in enumerate(group):
            put_qkv(i, term[:, 128 * n : 128 * n + 128])
    acc[:, 896:1024] = jnp.zeros((ROWS, 128), F32)
    acc[:, 0:D] = gn1
    gn1 = acc[...]
    n1 = xs[...].astype(F32) * inv1
    d_gain1 = jnp.sum(gn1 * n1, axis=0, keepdims=True)
    both_gains = jnp.concatenate([v[:, 128 * i : 128 * i + 128] for v in (d_gain1, d_gain2) for i in range(8)], axis=0)
    w[0, 0, 0, 0, 39] = both_gains.astype(BF)
    rs.offer(0)
    u = gn1 * gain1
    res = mid[...] + inv1 * (u - n1 * mean_of(u * n1))
    gin_ref[...] = res[:, 0:D].astype(BF)
    rs.first((0, 1))
    rs.finish()


def layer(block, inputs, cotangent, segments, counts):
    vm = pl.BlockSpec(memory_space=pltpu.VMEM)
    dma = pltpu.SemaphoreType.DMA
    return pl.pallas_call(
        layer_kernel,
        out_shape=(
            jax.ShapeDtypeStruct((ROWS, D), BF),
            jax.ShapeDtypeStruct((ROWS, D), BF),
            jax.ShapeDtypeStruct((TILES, 16, 128), F32),
        ),
        in_specs=[vm] * 7,
        out_specs=(vm, vm, vm),
        scratch_shapes=[
            pltpu.VMEM((4, 4, 4, 2, TILES, 16, 128), BF),
            pltpu.VMEM((3, 4, 4, TILES, 16, 128), BF),
            pltpu.VMEM((3, 4, 4, TILES, 16, 128), BF),
            pltpu.VMEM((3, 4, TILES, 16, 128), BF),
            pltpu.VMEM((3, TILES, 16, 128), BF),
            pltpu.VMEM((3, 4, TILES, 16, 128), BF),
            pltpu.VMEM((3, TILES, 16, 128), BF),
            pltpu.VMEM((3, 14, 16, 128), BF),
            pltpu.VMEM((ROWS, 1024), BF),
            pltpu.VMEM((ROWS, 1024), BF),
            pltpu.VMEM((ROWS, 1024), BF),
            pltpu.VMEM((8, ROWS, 128), BF),
            pltpu.VMEM((KV, ROWS, 128), BF),
            pltpu.VMEM((KV, ROWS, 128), BF),
            pltpu.VMEM((MB, KV, ROWS, MROWS), F32),
            pltpu.VMEM((ROWS, 1024), BF),
            pltpu.VMEM((ROWS, 1024), F32),
            pltpu.VMEM((ROWS, 1024), BF),
            pltpu.VMEM((4, ROWS, 640), BF),
            pltpu.VMEM((4, ROWS, 640), BF),
            pltpu.VMEM((4, ROWS, 640), BF),
            pltpu.VMEM((8, ROWS, 640), BF),
            pltpu.VMEM((13, ROWS, 128), F32),
            pltpu.VMEM((13, ROWS, 128), BF),
            pltpu.VMEM((8, 256, 128), BF),
            pltpu.VMEM((ROWS, 1024), F32),
            dma((99,)), dma((99,)), dma((91,)), dma((91,)), dma,
            dma((120,)), dma((120,)), dma((4,)), dma((4,)),
        ],
        compiler_params=pltpu.CompilerParams(collective_id=0, has_side_effects=True, vmem_limit_bytes=VMEM_BYTES),
    )(block, inputs, cotangent, *tables(segments, counts))


def shards(inputs, cotangent, flat_weights, counts, segments):
    d = lax.axis_index("fsdp")
    block_out, input_grad, block_grad = layer(to_block(flat_weights, d), inputs, cotangent, segments, counts)
    return block_out, input_grad, from_block(block_grad, d)


def solution(mesh):
    in_specs = (P("fsdp", None), P("fsdp", None), P("fsdp"), P("fsdp"), P("fsdp"))
    out_specs = (P("fsdp", None), P("fsdp", None), P("fsdp"))
    return jax.shard_map(shards, mesh=mesh, in_specs=in_specs, out_specs=out_specs, check_vma=False)
```

time: 189 us -> 175 us (0.926)
  Pallas kernels: 157 us -> 144 us
  other arithmetic: 6.99 us -> 4.69 us
    pallas_call x3 -> x1, Pallas kernels: 157 us -> 144 us  [layer(): pl.pallas_call(layer_kernel, out_shape=(jax.ShapeDtypeStruct((ROWS, D), B...]
    unnamed x4 -> x18, local copies, waits for them, and re-layouts: 0.21 us -> 4.25 us
  transfers between devices with their start and end apart: 2 -> 2, of which waited for: 1 -> 1; matrix products, arithmetic and copies ran while one was open for 3% -> 2% of each run, Pallas kernels for 0% -> 0%
where the time goes in v1:
time: 175 us; the launch traced here: 174 us
  Pallas kernels  144 us (82%)
  local copies, waits for them, and re-layouts  8.49 us (5%)
  starting transfers between devices  8.39 us (5%)
  waiting for transfers between devices  8.29 us (5%)
  other arithmetic  4.69 us (3%)
    pallas_call x1, Pallas kernels, layer(): pl.pallas_call(layer_kernel, out_shape=(jax.ShapeDtypeStruct((ROWS, D), B...  144 us
    ppermute x1, waiting for transfers between devices, from_block(): lax.ppermute(flat[BLOCK - GAINS:], 'fsdp', [(i, (i + 1) % N) for i in ran...  8.29 us
    ppermute x1, starting transfers between devices, to_block(): lax.ppermute(shard[:GAINS], 'fsdp', [(i, (i + N - 1) % N) for i in range(...  8.21 us
    unnamed x18, local copies, waits for them, and re-layouts  4.25 us
  transfers between devices with their start and end apart: 2, of which 1 were waited for; matrix products, arithmetic and copies ran while one was open for 2% of the time, Pallas kernels for 0%

profile of v1, /device:TPU:0, one launch (start us, length us, event | category | flops | bytes accessed | tf_op | source)
XLA Modules:
  0.0 174.4 jit_solution(3221758123741320339)
XLA Ops:
  0.6 0.7 slice.25
  1.3 8.2 %collective-permute-start = (bf16[1920]{0:T(1024)(128)(2,1)S(1)}, bf16[1920]{0:T(1024)(128)(2,1)S(1)}, u32[]{:S(2)}, u32[]{:S(2)}) collective-permute-start(bf16[1920]{0:T(1024)(128)(2,1)S(1)} %slice.25), channel_id=1, source_target_pairs={{0,127},{1,0},{2,1},{3,2},{4,3},{5,4},{6,5},{7,6},{8,7},{9,8},{10,... | collective-permute-start | bytes 11528 | tf_op jit(solution)/shard_map/ppermute | solution.py:195
  9.5 0.1 reshape.130
  9.7 0.7 copy-done.4
  10.3 0.1 eq.27
  10.4 0.2 select_reduce_fusion
  10.7 0.6 copy-done.5
  11.4 0.5 fusion.6
  11.9 1.0 pad_maximum_fusion
  12.9 0.8 fusion.5.bias_ref
  13.8 0.5 fusion.3
  14.2 0.2 reshape.127
  14.4 0.2 reshape.133
  14.5 0.1 reshape.131
  14.7 0.1 reshape.128
  15.0 0.8 fusion.2.blk
  15.8 0.7 broadcast_in_dim.41.live_ref
  16.5 143.7 %shard_map.76 = (bf16[240,960]{1,0:T(8,128)(2,1)}, bf16[240,960]{1,0:T(8,128)(2,1)}, f32[40,16,128]{2,1,0:T(8,128)}) custom-call(bf16[40,16,128]{2,1,0:T(8,128)(2,1)} %fusion.2.blk, bf16[240,960]{1,0:T(8,128)(2,1)} %x_ref.1, bf16[240,960]{1,0:T(8,128)(2,1)} %c_ref.1, f32[240,128]{1,0:T(8,128)} %get-tuple-element.12.cos_ref, ...), custom_call_target="tpu_custom_call" | custom-call | tf_op jit(solution)/shard_map/pallas_call | solution.py:787
  160.2 1.0 slice.28
  161.2 0.1 copy.18
  161.4 0.1 copy.29
  161.5 0.2 reshape.139
  161.7 0.8 copy-done
  162.4 0.1 copy.19
  162.5 0.1 copy.20
  162.7 0.2 reshape.143
  163.0 0.2 collective-permute-start.1
  163.3 8.3 %collective-permute-done.1 = f32[1920]{0:T(1024)S(1)} collective-permute-done((f32[1920]{0:T(1024)S(1)}, f32[1920]{0:T(1024)S(1)}, u32[]{:S(2)}, u32[]{:S(2)}) %collective-permute-start.1) | collective-permute-done | bytes 7712 | tf_op jit(solution)/shard_map/ppermute | solution.py:206
  171.6 0.9 fusion
  172.4 0.8 copy.32
  173.2 0.4 copy-done.1
  173.7 0.8 copy.33
  (30 shorter events, 0.7 us)
Async XLA Ops:
  1.3 12.4 %collective-permute-start = (bf16[1920]{0:T(1024)(128)(2,1)S(1)}, bf16[1920]{0:T(1024)(128)(2,1)S(1)}, u32[]{:S(2)}, u32[]{:S(2)}) collective-permute-start(bf16[1920]{0:T(1024)(128)(2,1)S(1)} %slice.25), channel_id=1, source_target_pairs={{0,127},{1,0},{2,1},{3,2},{4,3},{5,4},{6,5},{7,6},{8,7},{9,8},{10,... | collective-permute-start | bytes 11528 | tf_op jit(solution)/shard_map/ppermute | solution.py:195
  9.6 0.7 copy-start.4
  10.6 0.7 copy-start.5
  12.8 0.9 copy-start.3
  161.5 1.0 copy-start
  163.0 9.5 %copy-start.2 = (bf16[240,960]{1,0:T(8,128)(2,1)S(1)}, bf16[240,960]{1,0:T(8,128)(2,1)}, u32[]{:S(2)}) copy-start(bf16[240,960]{1,0:T(8,128)(2,1)} %get-tuple-element.17) | copy-start | bytes 1382404
  163.0 8.6 %collective-permute-start.1 = (f32[1920]{0:T(1024)S(1)}, f32[1920]{0:T(1024)S(1)}, u32[]{:S(2)}, u32[]{:S(2)}) collective-permute-start(f32[1920]{0:T(1024)S(1)} %slice.37), channel_id=1, source_target_pairs={{0,1},{1,2},{2,3},{3,4},{4,5},{5,6},{6,7},{7,8},{8,9},{9,10},{10,1... | collective-permute-start | bytes 23048 | tf_op jit(solution)/shard_map/ppermute | solution.py:206
  172.4 1.2 copy-start.1

commit v2 on v1

--- a/solution.py
+++ b/solution.py
@@ -42,13 +42,19 @@
     return out
 
 
+def beside(by):
+    return (lax.axis_index("fsdp") + by) % N
+
+
 def greet(coords, core):
     barrier = pltpu.get_barrier_semaphore()
     for dim in range(3):
         for by in (1, -1, 2):
             pl.semaphore_signal(barrier, inc=1, device_id=device_at(moved(coords, dim, by), core), device_id_type=MESH)
     pl.semaphore_signal(barrier, inc=1, device_id=device_at(coords, 1 - core), device_id_type=MESH)
-    pl.semaphore_wait(barrier, 10)
+    for by in (1, N - 1):
+        pl.semaphore_signal(barrier, inc=1, device_id=(beside(by),), device_id_type=MESH)
+    pl.semaphore_wait(barrier, 12)
 
 
 def gather_into(w, blk, coords, core, send, recv, pair_send, pair_recv, own_sem):
@@ -188,22 +194,41 @@
     qkv = jnp.concatenate([qkv, jnp.where(d == 0, gains, jnp.zeros_like(gains))[None]], axis=0)
     square = jnp.pad(rows_80, ((0, 0), (0, 64))).reshape(5, 16, 8, 128).transpose(2, 0, 1, 3).reshape(40, 16, 128)
     wide = jnp.pad(rows_15, ((0, 1), (0, 0))).reshape(16, 40, 128).transpose(1, 0, 2)
+    return kind(d, qkv, square, wide)
+
+
+def kind(d, qkv, square, wide):
     return jnp.where(d < 20, qkv, jnp.where((d >= 32) & (d < 96), wide, square))
 
 
 def to_block(shard, d):
-    following = lax.ppermute(shard[:GAINS], "fsdp", [(i, (i + N - 1) % N) for i in range(N)])
-    flat = lax.dynamic_slice(jnp.concatenate([shard, following]), (GAINS - 15 * d,), (BLOCK,))
+    none = jnp.zeros((GAINS,), BF)
+    flat = lax.dynamic_slice(jnp.concatenate([shard, none]), (GAINS - 15 * d,), (BLOCK,))
     gains = jnp.pad(shard[:GAINS].reshape(2, D), ((0, 0), (0, 64))).reshape(16, 128)
-    return pack(flat.reshape(48, 1600), flat.reshape(80, D), flat.reshape(15, 2 * FF), gains, d)
-
-
-def from_block(tiles, d):
+    block = pack(flat.reshape(48, 1600), flat.reshape(80, D), flat.reshape(15, 2 * FF), gains, d)
+    e = (d + N - 1) % N
+    last = lax.dynamic_slice(jnp.concatenate([none, shard[:GAINS]]), (GAINS - 15 - 15 * e,), (GAINS,))
+    qkv = jnp.stack([jnp.pad(last[:320], (1280, 64)).reshape(13, 128), jnp.pad(last[320:], (0, 64)).reshape(13, 128)], axis=1)
+    qkv = jnp.pad(jnp.pad(qkv[:, None], ((0, 0), (2, 0), (0, 0), (0, 0))).reshape(39, 2, 128), ((0, 1), (0, 0), (0, 0)))
+    square = jnp.pad(last.reshape(2, D), ((0, 0), (0, 64))).reshape(2, 8, 128).transpose(1, 0, 2)
+    square = jnp.pad(square[:, None], ((0, 0), (4, 0), (0, 0), (0, 0))).reshape(40, 2, 128)
+    wide = jnp.pad(last.reshape(15, 1, 128), ((25, 0), (0, 1), (0, 0)))
+    return block, kind(e, qkv, square, wide).reshape(5, 16, 128)
+
+
+def from_block(rows, prev, d):
+    tiles = rows.reshape(40, 16, 128)
     qkv = tiles[:39].reshape(13, 3, 16, 128).transpose(1, 2, 0, 3).reshape(48, 1664)[:, :1600].reshape(-1)
     square = tiles.reshape(8, 5, 16, 128).transpose(1, 2, 0, 3).reshape(80, 1024)[:, :D].reshape(-1)
     wide = tiles.transpose(1, 0, 2)[:15].reshape(-1)
-    flat = jnp.where(d < 20, qkv, jnp.where((d >= 32) & (d < 96), wide, square))
-    before = lax.ppermute(flat[BLOCK - GAINS :], "fsdp", [(i, (i + 1) % N) for i in range(N)])
+    flat = kind(d, qkv, square, wide)
+    two = prev[:, 2:39:3].reshape(2, 1664)
+    before = kind(
+        d - 1,
+        jnp.concatenate([two[0, 1280:1600], two[1, :1600]]),
+        prev[:, 4::5].reshape(2, 1024)[:, :D].reshape(-1),
+        prev[0, 25:].reshape(-1),
+    )
     before = jnp.where(d == 0, tiles[39].reshape(2, 1024)[:, :D].reshape(-1), before)
     return lax.dynamic_slice(jnp.concatenate([before, flat]), (15 * d,), (BLOCK + 15,))
 
@@ -254,37 +279,38 @@
         self.send, self.recv, self.pair_send, self.pair_recv = send, recv, pair_send, pair_recv
         self.sent, self.ids = [], {}
         b1, b2, b3, q1, q2, z2 = bufs
-        self.P0 = Flow("P0", (0, 1, 2), (0, 5, 10), (b1, b2, b3), 0)
-        self.P1 = Flow("P1", (1, 2, 0), (10, 17, 25), (b1, b2, None), 0)
-        self.P2 = Flow("P2", (2, 1, 0), (25, 32, 40), (b1, b2, None), 0)
+        self.P0 = Flow("P0", (0, 1, 2), (0, 4, 8), (b1, b2, b3), 0)
+        self.P1 = Flow("P1", (1, 2, 0), (8, 16, 24), (b1, b2, None), 0)
+        self.P2 = Flow("P2", (2, 1, 0), (24, 32, 40), (b1, b2, None), 0)
         self.Q1 = Flow("Q1", (1, 2, 0), (0, 10, 20), (q1, q2, None), 0)
         self.Q2 = Flow("Q2", (2, 1, 0), (20, 30, 40), (q1, q2, None), 0)
-        self.Z1 = Flow("Z1", (1, 2, 0), (10, 25, 40), (None, None, b3), 0)
-        self.Z2 = Flow("Z2", (1, 2, 0), (0, 5, 10), (None, None, z2), 0)
+        self.Z1 = Flow("Z1", (1, 2, 0), (8, 24, 40), (None, None, b3), 0)
+        self.Z2 = Flow("Z2", (1, 2, 0), (0, 4, 8), (None, None, z2), 0)
 
     def copy(self, src, dst, device, ssem, rsem):
         return pltpu.make_async_remote_copy(
             src_ref=src, dst_ref=dst, send_sem=ssem, recv_sem=rsem, device_id=device, device_id_type=MESH
         )
 
-    def offer(self, z):
+    def offer(self, k, z, tiles=(0, TILES), xs=(0, 4)):
+        x, t = rng(xs), rng(tiles)
         one = self.copy(
-            self.w.at[z, :, :, 1 - self.core], self.pair_buf.at[z % 3], device_at(self.coords, 1 - self.core),
-            self.pair_send.at[z], self.pair_recv.at[z],
+            self.w.at[z, x, :, 1 - self.core, t], self.pair_buf.at[z % 3, x, :, t],
+            device_at(self.coords, 1 - self.core), self.pair_send.at[k], self.pair_recv.at[k],
         )
         one.start()
         self.sent.append((None, one))
 
-    def ready(self, z):
-        slot = z % 3
-        landed(self.pair_buf.at[slot], self.pair_recv.at[z])
+    def ready(self, k, z, tiles=(0, TILES), xs=(0, 4)):
+        slot, span = z % 3, rng(tiles)
+        landed(self.pair_buf.at[slot, rng(xs), :, span], self.pair_recv.at[k])
 
         def body(t, _):
-            at = (z, t // 4, t % 4, self.core)
-            self.w[at] = self.w[at] + self.pair_buf[slot, t // 4, t % 4]
+            at = (z, xs[0] + t // 4, t % 4, self.core, span)
+            self.w[at] = self.w[at] + self.pair_buf[slot, xs[0] + t // 4, t % 4, span]
             return 0
 
-        lax.fori_loop(0, 16, body, 0)
+        lax.fori_loop(0, 4 * (xs[1] - xs[0]), body, 0)
 
     def sem(self, flow, phase, planes, sign, number):
         return self.ids.setdefault((flow.name, phase, planes, sign, number), len(self.ids))
@@ -382,7 +408,7 @@
         def total(at, inner):
             value = self.w[(*at, tiles)].astype(F32) + buf[(0, *inner, tiles)].astype(F32) + buf[(1, *inner, tiles)].astype(F32)
             if phase == 2:
-                self.red[tiles] = value
+                self.red[pl.ds(16 * flow.tiles[0], 16 * (flow.tiles[2] - flow.tiles[0])), :] = value.reshape(-1, 128)
             else:
                 self.w[(*at, tiles)] = value.astype(BF)
 
@@ -392,28 +418,25 @@
         z = self.along(0, step)
         return (z >= planes[0]) & (z < planes[1])
 
-    def first(self, planes):
-        for z in range(*planes):
-            self.ready(z)
-        flows = (self.P1, self.P2) if planes[0] else (self.Q1, self.Q2)
+    def open(self, planes, flows, along_z=False):
         for number in (0, 1):
             for sign in (1, -1):
                 for flow in flows:
                     self.go(flow, 0, planes, sign, number)
-                if planes[0]:
+                if along_z:
                     one = self.ship(self.P0, 0, (0, 4), sign, number)
                     pl.when(self.plane_in(planes, 2 if number == 0 else sign))(one.start)
 
-    def second(self, planes):
-        for sign in (1, -1):
-            if planes[0]:
+    def relay(self, planes, flows, along_z=False):
+        for sign in (1, -1):
+            if along_z:
 
                 @pl.when(self.plane_in(planes, sign))
                 def _():
                     self.add_half(self.P0, 0, (0, 4), sign)
                     self.ship(self.P0, 0, (0, 4), sign, 2).start()
 
-            for flow in (self.P1, self.P2) if planes[0] else (self.Q1, self.Q2):
+            for flow in flows:
                 self.add_half(flow, 0, planes, sign)
                 self.go(flow, 0, planes, sign, 2)
 
@@ -476,7 +499,7 @@
             for slot in range(3):
                 value = value + buf[(slot, *inner, tiles)].astype(F32)
             if phase == 2:
-                self.red[tiles] = value
+                self.red[pl.ds(16 * flow.tiles[0], 16 * (flow.tiles[2] - flow.tiles[0])), :] = value.reshape(-1, 128)
             else:
                 self.w[(*at, tiles)] = value.astype(BF)
 
@@ -495,7 +518,7 @@
             for planes in ((3, 4), (1, 3)):
                 self.add_all(flow, 0, planes)
             self.start(flow, 1, early)
-        self.second(late)
+        self.relay(late, (self.Q1, self.Q2))
         pl.when(z != 0)(lambda: self.add_all(self.P0, 0, every))
         self.start(self.P0, 1, every, upper)
         for flow in (self.P1, self.P2):
@@ -515,6 +538,8 @@
         self.add_direct(self.Z1, 2, every)
         pl.when(z != 0)(lambda: self.add_direct(self.P0, 2, every))
         pl.when(z == 0)(lambda: self.add_direct(self.Z2, 2, every))
+
+    def drain(self):
         for guard, one in self.sent:
             if guard is None:
                 one.wait_send()
@@ -531,13 +556,23 @@
 
 
 def layer_kernel(
-    blk, x_ref, c_ref, cos_ref, sin_ref, bias_ref, live_ref,
-    out_ref, gin_ref, red_ref,
-    w, pair_buf, b1, b2, b3, q1, q2, z2, xs, go, nrm, qs, kk, vv, prob, mixed, mid, n2p, gate, up, hid, ggu, gq, gqb, spread, acc,
+    own_ref, tail_ref, x_ref, c_ref, cos_ref, sin_ref, bias_ref, live_ref,
+    out_ref, gin_ref, red_ref, prev_ref,
+    blk, tail_in, tail_out, tail_back, tail_sem, w, pair_buf, b1, b2, b3, q1, q2, z2, xs, go, nrm, qs, kk, vv, prob, mixed, mid, n2p, gate, up, hid, ggu, gq, gqb, spread, acc,
     send, recv, pair_send, pair_recv, own_sem, rs_send, rs_recv, rp_send, rp_recv,
 ):
     coords, core = place()
     greet(coords, core)
+    handed = pltpu.make_async_remote_copy(
+        src_ref=tail_ref, dst_ref=tail_in, send_sem=tail_sem.at[0], recv_sem=tail_sem.at[1],
+        device_id=(beside(N - 1),), device_id_type=MESH,
+    )
+    handed.start()
+    r = lax.broadcasted_iota(jnp.int32, (640, 80), 0)
+    c = lax.broadcasted_iota(jnp.int32, (640, 80), 1)
+    last_rows = jnp.where((r // 16 == c // 2) & (r % 16 == 14 + c % 2), 1.0, 0.0).astype(BF)
+    handed.wait()
+    blk[...] = own_ref[...] + dot(last_rows, tail_in[...].reshape(80, 128)).astype(BF).reshape(TILES, 16, 128)
     sent = gather_into(w, blk, coords, core, send, recv, pair_send, pair_recv, own_sem)
     rs = Reduce(w, pair_buf, (b1, b2, b3, q1, q2, z2), red_ref, coords, core, rs_send, rs_recv, rp_send, rp_recv)
 
@@ -637,7 +672,7 @@
             s = dot(q, kk[g, rows, :], 1, 1) * 0.125 + bias3
             e = jnp.exp(s - jnp.max(s, axis=-1, keepdims=True))
             p = e / jnp.sum(e, axis=-1, keepdims=True)
-            prob[m, g] = p
+            prob[m, g] = p.astype(BF)
             o = dot(p.astype(BF), vv[g, rows, :]).astype(BF)
             for i, h in enumerate(heads):
                 mixed[rows, chunk(h)] = jnp.where(half[h % 2], o[MROWS * i : MROWS * i + MROWS], mixed[rows, chunk(h)])
@@ -683,8 +718,10 @@
                 w[3, c, :, :, 5 * (i + n) : 5 * (i + n) + 5] = term[:, 128 * n : 128 * n + 128].reshape(4, 2, 5, 16, 128)
         return 0
 
-    lax.fori_loop(0, 4, reduce_, 0)
-    rs.offer(3)
+    lax.fori_loop(0, 2, reduce_, 0)
+    rs.offer(0, 3, xs=(0, 2))
+    lax.fori_loop(2, 4, reduce_, 0)
+    rs.offer(1, 3, xs=(2, 4))
     out_ref[...] = (acc[:, 0:D] * live).astype(BF)
 
     acc[...] = jnp.zeros((ROWS, 1024), F32)
@@ -698,12 +735,20 @@
                 w[1:3, :, :, :, 5 * c + i + n] = term[:, 128 * n : 128 * n + 128].reshape(2, 4, 4, 2, 16, 128)
         return 0
 
-    lax.fori_loop(0, 4, back, 0)
-    rs.first((3, 4))
-    lax.fori_loop(4, 8, back, 0)
-    rs.offer(1)
-    rs.offer(2)
-    rs.second((3, 4))
+    lax.fori_loop(0, 2, back, 0)
+    rs.ready(0, 3, xs=(0, 2))
+    rs.ready(1, 3, xs=(2, 4))
+    rs.open((3, 4), (rs.P1, rs.P2), True)
+    lax.fori_loop(2, 5, back, 0)
+    rs.offer(2, 1, (0, 25))
+    rs.offer(3, 2, (0, 25))
+    lax.fori_loop(5, 8, back, 0)
+    rs.offer(4, 1, (25, 40))
+    rs.offer(5, 2, (25, 40))
+    rs.relay((3, 4), (rs.P1, rs.P2), True)
+    rs.ready(2, 1, (0, 25))
+    rs.ready(3, 2, (0, 25))
+    rs.open((1, 3), (rs.P1,), True)
     gn = acc[...]
     hi = gn.astype(BF)
     lo = (gn - hi.astype(F32)).astype(BF)
@@ -726,7 +771,9 @@
     term = dot(mixed[:, 0:D], gmb, 0, 0).astype(BF)
     for i in range(8):
         put_out(i, term[:, 128 * i : 128 * i + 128])
-    rs.first((1, 3))
+    rs.ready(4, 1, (25, 40))
+    rs.ready(5, 2, (25, 40))
+    rs.open((1, 3), (rs.P2,))
     mixed[:, 0:D] = gmix.astype(BF)
     gq[12] = jnp.zeros((ROWS, 128), F32)
 
@@ -736,8 +783,8 @@
             heads = [3 * g + i for i in range(3)]
             q = jnp.concatenate([jnp.where(half[h % 2], qs[h // 2, rows, :], zero_b) for h in heads], axis=0)
             gmx = jnp.concatenate([jnp.where(half[h % 2], mixed[rows, chunk(h)], zero_b) for h in heads], axis=0)
-            p = prob[m, g]
-            gv = dot(p.astype(BF), gmx, 0, 0)
+            gv = dot(prob[m, g], gmx, 0, 0)
+            p = prob[m, g].astype(F32)
             gp = dot(gmx, vv[g, rows, :], 1, 1)
             gs = (p * (gp - jnp.sum(p * gp, axis=-1, keepdims=True))).astype(BF)
             gqs = dot(gs, kk[g, rows, :]) * 0.125
@@ -749,8 +796,10 @@
                 gq[head // 2, rows, :] = jnp.where(half[head % 2], value, gq[head // 2, rows, :])
         return 0
 
-    lax.fori_loop(0, 2, attend_back, 0)
-    rs.second((1, 3))
+    lax.fori_loop(0, 1, attend_back, 0)
+    rs.relay((1, 3), (rs.P1,), True)
+    lax.fori_loop(1, 2, attend_back, 0)
+    rs.relay((1, 3), (rs.P2,))
     lax.fori_loop(2, MB, attend_back, 0)
 
     for c in range(13):
@@ -773,15 +822,29 @@
     d_gain1 = jnp.sum(gn1 * n1, axis=0, keepdims=True)
     both_gains = jnp.concatenate([v[:, 128 * i : 128 * i + 128] for v in (d_gain1, d_gain2) for i in range(8)], axis=0)
     w[0, 0, 0, 0, 39] = both_gains.astype(BF)
-    rs.offer(0)
+    rs.offer(6, 0, (0, 20))
+    rs.offer(7, 0, (20, 40))
     u = gn1 * gain1
     res = mid[...] + inv1 * (u - n1 * mean_of(u * n1))
     gin_ref[...] = res[:, 0:D].astype(BF)
-    rs.first((0, 1))
+    rs.ready(6, 0, (0, 20))
+    rs.open((0, 1), (rs.Q1,))
+    rs.ready(7, 0, (20, 40))
+    rs.open((0, 1), (rs.Q2,))
     rs.finish()
-
-
-def layer(block, inputs, cotangent, segments, counts):
+    for n in range(2):
+        tail_out[n] = red_ref[pl.ds(14 + n, TILES, stride=16), :]
+    handed = pltpu.make_async_remote_copy(
+        src_ref=tail_out, dst_ref=tail_back, send_sem=tail_sem.at[2], recv_sem=tail_sem.at[3],
+        device_id=(beside(1),), device_id_type=MESH,
+    )
+    handed.start()
+    rs.drain()
+    handed.wait()
+    prev_ref[...] = tail_back[...]
+
+
+def layer(block, tail, inputs, cotangent, segments, counts):
     vm = pl.BlockSpec(memory_space=pltpu.VMEM)
     dma = pltpu.SemaphoreType.DMA
     return pl.pallas_call(
@@ -789,11 +852,17 @@
         out_shape=(
             jax.ShapeDtypeStruct((ROWS, D), BF),
             jax.ShapeDtypeStruct((ROWS, D), BF),
-            jax.ShapeDtypeStruct((TILES, 16, 128), F32),
+            jax.ShapeDtypeStruct((TILES * 16, 128), F32),
+            jax.ShapeDtypeStruct((2, TILES, 128), F32),
         ),
-        in_specs=[vm] * 7,
-        out_specs=(vm, vm, vm),
+        in_specs=[vm] * 8,
+        out_specs=(vm, vm, vm, vm),
         scratch_shapes=[
+            pltpu.VMEM((TILES, 16, 128), BF),
+            pltpu.VMEM((5, 16, 128), BF),
+            pltpu.VMEM((2, TILES, 128), F32),
+            pltpu.VMEM((2, TILES, 128), F32),
+            dma((4,)),
             pltpu.VMEM((4, 4, 4, 2, TILES, 16, 128), BF),
             pltpu.VMEM((3, 4, 4, TILES, 16, 128), BF),
             pltpu.VMEM((3, 4, 4, TILES, 16, 128), BF),
@@ -808,7 +877,7 @@
             pltpu.VMEM((8, ROWS, 128), BF),
             pltpu.VMEM((KV, ROWS, 128), BF),
             pltpu.VMEM((KV, ROWS, 128), BF),
-            pltpu.VMEM((MB, KV, ROWS, MROWS), F32),
+            pltpu.VMEM((MB, KV, ROWS, MROWS), BF),
             pltpu.VMEM((ROWS, 1024), BF),
             pltpu.VMEM((ROWS, 1024), F32),
             pltpu.VMEM((ROWS, 1024), BF),
@@ -821,16 +890,17 @@
             pltpu.VMEM((8, 256, 128), BF),
             pltpu.VMEM((ROWS, 1024), F32),
             dma((99,)), dma((99,)), dma((91,)), dma((91,)), dma,
-            dma((120,)), dma((120,)), dma((4,)), dma((4,)),
+            dma((120,)), dma((120,)), dma((8,)), dma((8,)),
         ],
         compiler_params=pltpu.CompilerParams(collective_id=0, has_side_effects=True, vmem_limit_bytes=VMEM_BYTES),
-    )(block, inputs, cotangent, *tables(segments, counts))
+    )(block, tail, inputs, cotangent, *tables(segments, counts))
 
 
 def shards(inputs, cotangent, flat_weights, counts, segments):
     d = lax.axis_index("fsdp")
-    block_out, input_grad, block_grad = layer(to_block(flat_weights, d), inputs, cotangent, segments, counts)
-    return block_out, input_grad, from_block(block_grad, d)
+    block, tail = to_block(flat_weights, d)
+    block_out, input_grad, rows, prev = layer(block, tail, inputs, cotangent, segments, counts)
+    return block_out, input_grad, from_block(rows, prev, d)
 
 
 def solution(mesh):

time: 175 us -> 168 us (0.960)
  starting transfers between devices: 8.39 us -> 0 us
  waiting for transfers between devices: 8.29 us -> 0 us
  Pallas kernels: 144 us -> 150 us
  local copies, waits for them, and re-layouts: 8.49 us -> 11 us
    ppermute x2 -> x0, starting transfers between devices: 8.39 us -> none  [the longest x1 8.21 us: to_block(): lax.ppermute(shard[:GAINS], 'fsdp', [(i, (i + N - 1) % N) for i in range(...]
    ppermute x2 -> x0, waiting for transfers between devices: 8.29 us -> none  [the longest x1 8.29 us: from_block(): lax.ppermute(flat[BLOCK - GAINS:], 'fsdp', [(i, (i + 1) % N) for i in ran...]
    pallas_call x1, Pallas kernels: 144 us -> 150 us  [layer(): pl.pallas_call(layer_kernel, out_shape=(jax.ShapeDtypeStruct((ROWS, D), B...]
    unnamed x18 -> x26, local copies, waits for them, and re-layouts: 4.25 us -> 4.4 us
  transfers between devices with their start and end apart: 2 -> 0, of which waited for: 1 -> 0; matrix products, arithmetic and copies ran while one was open for 2% -> 0% of each run, Pallas kernels for 0% -> 0%
where the time goes in v2:
time: 168 us; the launch traced here: 167 us
  Pallas kernels  150 us (89%)
  local copies, waits for them, and re-layouts  11 us (7%)
  other arithmetic  5.07 us (3%)
    pallas_call x1, Pallas kernels, layer(): pl.pallas_call(layer_kernel, out_shape=(jax.ShapeDtypeStruct((ROWS, D), B...  150 us
    unnamed x26, local copies, waits for them, and re-layouts  4.4 us

profile of v2, /device:TPU:0, one launch (start us, length us, event | category | flops | bytes accessed | tf_op | source)
XLA Modules:
  0.0 167.0 jit_solution(5862183658357696506)
XLA Ops:
  0.7 0.7 copy-done.5
  1.4 0.2 select_reduce_fusion
  1.8 0.6 copy-done.6
  2.5 0.7 slice.48
  3.9 0.7 broadcast_select_fusion.1
  4.6 0.8 fusion.4.bias_ref
  5.3 0.7 broadcast_in_dim.50.live_ref
  6.1 0.2 pad_dynamic-slice_fusion.2
  6.3 0.2 reshape.158
  6.5 0.1 reshape.159
  6.7 0.2 reshape.164
  6.9 0.1 reshape.162
  7.1 0.8 fusion.2.own_ref
  7.8 0.5 fusion.5
  8.3 1.0 pad_maximum_fusion
  9.3 150.0 %shard_map.76 = (bf16[240,960]{1,0:T(8,128)(2,1)}, bf16[240,960]{1,0:T(8,128)(2,1)}, f32[640,128]{1,0:T(8,128)}, f32[2,40,128]{2,1,0:T(8,128)}) custom-call(bf16[40,16,128]{2,1,0:T(8,128)(2,1)} %fusion.2.own_ref, bf16[5,16,128]{2,1,0:T(8,128)(2,1)} %bitcast.104, bf16[240,960]{1,0:T(8,128)(2,1)} %x_ref.1, bf16[240,960]{1,0:T(8,128)(2,1)} %c_ref.1, ...), custom_call_target="tpu_custom_call" | custom-call | tf_op jit(solution)/shard_map/pallas_call | solution.py:850
  159.3 0.8 slice.57
  160.2 0.7 slice.51
  161.2 1.0 slice.59
  162.2 0.1 copy.31
  162.3 0.1 copy.52
  162.4 0.2 reshape.179
  162.6 0.8 copy-done
  163.4 0.1 copy.51
  163.5 0.1 copy.33
  163.7 0.2 reshape.183
  163.9 0.1 select_select_fusion
  164.0 0.9 fusion
  164.9 0.1 copy-done.2
  165.0 0.8 copy.58
  165.8 0.4 copy-done.1
  166.2 0.8 copy.59
  (50 shorter events, 1.6 us)
Async XLA Ops:
  0.7 0.7 copy-start.5
  1.7 0.7 copy-start.6
  3.9 2.2 %copy-start.3 = (bf16[76815]{0:T(1024)(128)(2,1)S(1)}, bf16[76815]{0:T(1024)(128)(2,1)}, u32[]{:S(2)}) copy-start(bf16[76815]{0:T(1024)(128)(2,1)} %param.7) | copy-start | bytes 460894
  160.1 0.9 copy-start.4
  162.4 1.0 copy-start
  164.0 1.0 copy-start.2
  165.0 1.2 copy-start.1

commit v3 on v2

--- a/solution.py
+++ b/solution.py
@@ -251,7 +251,7 @@
     allowed = same & (places[None, None, :] <= places[None, :, None])
     bias = jnp.where(allowed, 0.0, -1e30).astype(F32).reshape(ROWS, MROWS)
     live = (places[None, :] < counts[:, None]).astype(F32).reshape(ROWS, 1)
-    return cos_t, sin_t, bias, jnp.broadcast_to(live, (ROWS, 128))
+    return cos_t, sin_t, jnp.concatenate([bias, jnp.broadcast_to(live, (ROWS, 48))], axis=1)
 
 
 def dot(a, b, ca=1, cb=0):
@@ -556,7 +556,7 @@
 
 
 def layer_kernel(
-    own_ref, tail_ref, x_ref, c_ref, cos_ref, sin_ref, bias_ref, live_ref,
+    own_ref, tail_ref, x_ref, c_ref, cos_ref, sin_ref, bias_ref,
     out_ref, gin_ref, red_ref, prev_ref,
     blk, tail_in, tail_out, tail_back, tail_sem, w, pair_buf, b1, b2, b3, q1, q2, z2, xs, go, nrm, qs, kk, vv, prob, mixed, mid, n2p, gate, up, hid, ggu, gq, gqb, spread, acc,
     send, recv, pair_send, pair_recv, own_sem, rs_send, rs_recv, rp_send, rp_recv,
@@ -571,6 +571,20 @@
     r = lax.broadcasted_iota(jnp.int32, (640, 80), 0)
     c = lax.broadcasted_iota(jnp.int32, (640, 80), 1)
     last_rows = jnp.where((r // 16 == c // 2) & (r % 16 == 14 + c % 2), 1.0, 0.0).astype(BF)
+    for k in range(8):
+        r = lax.broadcasted_iota(jnp.int32, (256, 128), 0) + 128 * (k - 1)
+        c = lax.broadcasted_iota(jnp.int32, (256, 128), 1) + 128 * k
+        spread[k] = jnp.where((r == (c // 16) * 15 + c % 16) & (c % 16 != 15), 1.0, 0.0).astype(BF)
+
+    xs[:, 896:1024] = jnp.zeros((ROWS, 128), BF)
+    xs[:, 0:D] = x_ref[...]
+    go[:, 896:1024] = jnp.zeros((ROWS, 128), BF)
+    live = bias_ref[:, MROWS : MROWS + 1]
+    go[:, 0:D] = (c_ref[...].astype(F32) * live).astype(BF)
+    x = xs[...].astype(F32)
+    inv1 = lax.rsqrt(mean_of(x * x) + EPSILON)
+    mixed[:, 896:1024] = jnp.zeros((ROWS, 128), BF)
+    gq[12] = jnp.zeros((ROWS, 128), F32)
     handed.wait()
     blk[...] = own_ref[...] + dot(last_rows, tail_in[...].reshape(80, 128)).astype(BF).reshape(TILES, 16, 128)
     sent = gather_into(w, blk, coords, core, send, recv, pair_send, pair_recv, own_sem)
@@ -619,22 +633,10 @@
         other = pltpu.roll(v, 64, 1)
         return jnp.where(low_all, v, other) if h == 0 else jnp.where(low_all, other, v)
 
-    for k in range(8):
-        r = lax.broadcasted_iota(jnp.int32, (256, 128), 0) + 128 * (k - 1)
-        c = lax.broadcasted_iota(jnp.int32, (256, 128), 1) + 128 * k
-        spread[k] = jnp.where((r == (c // 16) * 15 + c % 16) & (c % 16 != 15), 1.0, 0.0).astype(BF)
-
-    xs[:, 896:1024] = jnp.zeros((ROWS, 128), BF)
-    xs[:, 0:D] = x_ref[...]
-    go[:, 896:1024] = jnp.zeros((ROWS, 128), BF)
-    live = live_ref[:, 0:1]
-    go[:, 0:D] = (c_ref[...].astype(F32) * live).astype(BF)
-    x = xs[...].astype(F32)
-    inv1 = lax.rsqrt(mean_of(x * x) + EPSILON)
     gains = w[0, 0, 0, 0, 39].astype(F32)
     gain1 = side([gains[i : i + 1] for i in range(8)])
     gain2 = side([gains[8 + i : 9 + i] for i in range(8)])
-    nrm[...] = (x * inv1 * gain1).astype(BF)
+    nrm[...] = (xs[...].astype(F32) * inv1 * gain1).astype(BF)
 
     cos_t, sin_t = cos_ref[...], sin_ref[...]
     for c in range(0, 13, 2):
@@ -653,7 +655,6 @@
                 if 20 <= head < 25:
                     vv[head - 20] = both(y, h).astype(BF)
 
-    mixed[:, 896:1024] = jnp.zeros((ROWS, 128), BF)
     zero_b = jnp.zeros((MROWS, 128), BF)
 
     def rows_of(m):
@@ -664,7 +665,7 @@
 
     def attend(m, _):
         rows = rows_of(m)
-        bias = bias_ref[rows, :]
+        bias = bias_ref[rows, 0:MROWS]
         bias3 = jnp.concatenate([bias, bias, bias], axis=0)
         for g in range(KV):
             heads = [3 * g + i for i in range(3)]
@@ -775,7 +776,6 @@
     rs.ready(5, 2, (25, 40))
     rs.open((1, 3), (rs.P2,))
     mixed[:, 0:D] = gmix.astype(BF)
-    gq[12] = jnp.zeros((ROWS, 128), F32)
 
     def attend_back(m, _):
         rows = rows_of(m)
@@ -855,7 +855,7 @@
             jax.ShapeDtypeStruct((TILES * 16, 128), F32),
             jax.ShapeDtypeStruct((2, TILES, 128), F32),
         ),
-        in_specs=[vm] * 8,
+        in_specs=[vm] * 7,
         out_specs=(vm, vm, vm, vm),
         scratch_shapes=[
             pltpu.VMEM((TILES, 16, 128), BF),

time: 168 us -> 167 us (level)
  no operation moved by 1% of the time
where the time goes in v3:
time: 167 us; the launch traced here: 166 us
  Pallas kernels  150 us (90%)
  local copies, waits for them, and re-layouts  10.4 us (6%)
  other arithmetic  5.17 us (3%)
    pallas_call x1, Pallas kernels, layer(): pl.pallas_call(layer_kernel, out_shape=(jax.ShapeDtypeStruct((ROWS, D), B...  150 us
    unnamed x26, local copies, waits for them, and re-layouts  4.54 us

profile of v3, /device:TPU:0, one launch (start us, length us, event | category | flops | bytes accessed | tf_op | source)
XLA Modules:
  0.0 166.4 jit_solution(15778712753418484956)
XLA Ops:
  0.7 0.7 copy-done.5
  1.4 0.2 select_reduce_fusion
  1.8 0.6 copy-done.6
  2.5 0.7 slice.48
  3.9 0.7 broadcast_select_fusion.1
  4.8 0.8 pad_maximum_fusion.2.bias_ref
  5.5 0.1 copy-done.3
  5.7 0.2 pad_dynamic-slice_fusion.2
  5.9 0.2 reshape.158
  6.1 0.1 reshape.159
  6.3 0.2 reshape.164
  6.5 0.1 reshape.162
  6.7 0.8 fusion.2.own_ref
  7.4 0.5 fusion.5
  8.0 1.0 pad_maximum_fusion
  8.9 149.8 %shard_map.76 = (bf16[240,960]{1,0:T(8,128)(2,1)}, bf16[240,960]{1,0:T(8,128)(2,1)}, f32[640,128]{1,0:T(8,128)}, f32[2,40,128]{2,1,0:T(8,128)}) custom-call(bf16[40,16,128]{2,1,0:T(8,128)(2,1)} %fusion.2.own_ref, bf16[5,16,128]{2,1,0:T(8,128)(2,1)} %bitcast.104, bf16[240,960]{1,0:T(8,128)(2,1)} %x_ref.1, bf16[240,960]{1,0:T(8,128)(2,1)} %c_ref.1, ...), custom_call_target="tpu_custom_call" | custom-call | tf_op jit(solution)/shard_map/pallas_call | solution.py:850
  158.8 0.8 slice.57
  159.6 0.7 slice.51
  160.6 1.0 slice.59
  161.6 0.1 copy.31
  161.7 0.1 copy.52
  161.8 0.2 reshape.179
  162.0 0.8 copy-done
  162.8 0.1 copy.51
  162.9 0.1 copy.33
  163.1 0.2 reshape.183
  163.3 0.1 select_select_fusion
  163.4 0.9 fusion
  164.3 0.1 copy-done.2
  164.4 0.8 copy.58
  165.2 0.4 copy-done.1
  165.6 0.8 copy.59
  (51 shorter events, 1.8 us)
Async XLA Ops:
  0.7 0.7 copy-start.5
  1.7 0.7 copy-start.6
  4.8 0.9 copy-start.3
  159.5 0.9 copy-start.4
  161.8 1.0 copy-start
  163.4 1.0 copy-start.2
  164.4 1.2 copy-start.1

commit v4 on v3

--- a/solution.py
+++ b/solution.py
@@ -775,6 +775,7 @@
     rs.ready(4, 1, (25, 40))
     rs.ready(5, 2, (25, 40))
     rs.open((1, 3), (rs.P2,))
+    rs.offer(8, 0, xs=(3, 4))
     mixed[:, 0:D] = gmix.astype(BF)
 
     def attend_back(m, _):
@@ -822,14 +823,15 @@
     d_gain1 = jnp.sum(gn1 * n1, axis=0, keepdims=True)
     both_gains = jnp.concatenate([v[:, 128 * i : 128 * i + 128] for v in (d_gain1, d_gain2) for i in range(8)], axis=0)
     w[0, 0, 0, 0, 39] = both_gains.astype(BF)
-    rs.offer(6, 0, (0, 20))
-    rs.offer(7, 0, (20, 40))
+    rs.offer(6, 0, (0, 20), (0, 3))
+    rs.offer(7, 0, (20, 40), (0, 3))
+    rs.ready(8, 0, xs=(3, 4))
     u = gn1 * gain1
     res = mid[...] + inv1 * (u - n1 * mean_of(u * n1))
     gin_ref[...] = res[:, 0:D].astype(BF)
-    rs.ready(6, 0, (0, 20))
+    rs.ready(6, 0, (0, 20), (0, 3))
     rs.open((0, 1), (rs.Q1,))
-    rs.ready(7, 0, (20, 40))
+    rs.ready(7, 0, (20, 40), (0, 3))
     rs.open((0, 1), (rs.Q2,))
     rs.finish()
     for n in range(2):
@@ -890,7 +892,7 @@
             pltpu.VMEM((8, 256, 128), BF),
             pltpu.VMEM((ROWS, 1024), F32),
             dma((99,)), dma((99,)), dma((91,)), dma((91,)), dma,
-            dma((120,)), dma((120,)), dma((8,)), dma((8,)),
+            dma((120,)), dma((120,)), dma((9,)), dma((9,)),
         ],
         compiler_params=pltpu.CompilerParams(collective_id=0, has_side_effects=True, vmem_limit_bytes=VMEM_BYTES),
     )(block, tail, inputs, cotangent, *tables(segments, counts))

time: 167 us -> 167 us (level)
  Pallas kernels: 150 us -> 148 us
where the time goes in v4:
time: 167 us; the launch traced here: 165 us
  Pallas kernels  148 us (89%)
  local copies, waits for them, and re-layouts  10.4 us (6%)
  other arithmetic  5.17 us (3%)
    pallas_call x1, Pallas kernels, layer(): pl.pallas_call(layer_kernel, out_shape=(jax.ShapeDtypeStruct((ROWS, D), B...  148 us
    unnamed x26, local copies, waits for them, and re-layouts  4.54 us

profile of v4, /device:TPU:0, one launch (start us, length us, event | category | flops | bytes accessed | tf_op | source)
XLA Modules:
  0.0 164.9 jit_solution(16761922975552328088)
XLA Ops:
  0.7 0.7 copy-done.5
  1.4 0.2 select_reduce_fusion
  1.8 0.6 copy-done.6
  2.5 0.7 slice.48
  3.9 0.7 broadcast_select_fusion.1
  4.8 0.8 pad_maximum_fusion.2.bias_ref
  5.5 0.1 copy-done.3
  5.7 0.2 pad_dynamic-slice_fusion.2
  5.9 0.2 reshape.158
  6.1 0.1 reshape.159
  6.3 0.2 reshape.164
  6.5 0.1 reshape.162
  6.7 0.8 fusion.2.own_ref
  7.4 0.5 fusion.5
  8.0 1.0 pad_maximum_fusion
  8.9 148.4 %shard_map.76 = (bf16[240,960]{1,0:T(8,128)(2,1)}, bf16[240,960]{1,0:T(8,128)(2,1)}, f32[640,128]{1,0:T(8,128)}, f32[2,40,128]{2,1,0:T(8,128)}) custom-call(bf16[40,16,128]{2,1,0:T(8,128)(2,1)} %fusion.2.own_ref, bf16[5,16,128]{2,1,0:T(8,128)(2,1)} %bitcast.104, bf16[240,960]{1,0:T(8,128)(2,1)} %x_ref.1, bf16[240,960]{1,0:T(8,128)(2,1)} %c_ref.1, ...), custom_call_target="tpu_custom_call" | custom-call | tf_op jit(solution)/shard_map/pallas_call | solution.py:852
  157.3 0.8 slice.57
  158.1 0.7 slice.51
  159.1 1.0 slice.59
  160.1 0.1 copy.31
  160.2 0.1 copy.52
  160.3 0.2 reshape.179
  160.5 0.8 copy-done
  161.3 0.1 copy.51
  161.4 0.1 copy.33
  161.6 0.2 reshape.183
  161.8 0.1 select_select_fusion
  161.9 0.9 fusion
  162.8 0.1 copy-done.2
  163.0 0.8 copy.58
  163.7 0.4 copy-done.1
  164.2 0.8 copy.59
  (51 shorter events, 1.8 us)
Async XLA Ops:
  0.7 0.7 copy-start.5
  1.7 0.7 copy-start.6
  4.8 0.9 copy-start.3
  158.1 0.9 copy-start.4
  160.3 1.0 copy-start
  161.9 1.0 copy-start.2
  163.0 1.2 copy-start.1
